TPU v7x, 256 devices: a whole 4x4x8 slice. The times are simulated.
256 devices in a mesh: context: 16 (over y, x), tensor: 16 (over z, core).
Axes of the slice: x: 4, y: 4, z: 8, core: 2. Of those that a mesh axis runs over, the one named last changes fastest.
Arguments:
- x_in: bfloat16 [4096, 8192], P('context', 'tensor'), may hold values from -6 to 6
- gate_in: bfloat16 [4096, 8192], P('context', 'tensor'), may hold values from -12 to 12
- b_in: bfloat16 [4096, 1024], P('context'), may hold values from -0.375 to 0.375
- c_in: bfloat16 [4096, 1024], P('context'), may hold values from -6 to 6
- dt_raw: float32 [128, 4096], P('tensor', 'context'), may hold values from -5 to 5
- dt_bias: float32 [128], P('tensor'), may hold values from -3 to -1
- a_log: float32 [128], P('tensor'), as said below
- skip_weight: float32 [128], P('tensor'), may hold values from 0.5 to 1.5
- norm_gain: float32 [8192], P('tensor'), may hold values from 0.5 to 1.5
- w_out: bfloat16 [8192, 8192], P('tensor'), may hold values from -0.0625 to 0.0625
- doc_starts: int32 [4], replicated, may hold values from 1 to 3968, as said below
- grad_out: bfloat16 [4096, 8192], P(('context', 'tensor')), may hold values from -6 to 6
Outputs:
- mixed_out: bfloat16 [4096, 8192], P(('context', 'tensor'))
- grad_x: bfloat16 [4096, 8192], P('context', 'tensor')
- grad_gate: bfloat16 [4096, 8192], P('context', 'tensor')
- grad_b: bfloat16 [4096, 1024], P('context', 'tensor')
- grad_c: bfloat16 [4096, 1024], P('context', 'tensor')
- grad_dt: float32 [128, 4096], P('tensor', 'context')
Inputs may be any that keep to these rules, and one draw needn't show every extreme that they name: `doc_starts`: 4 distinct positions in increasing order, the last of them 4096 - 256 / 2; position 0 begins a document as well. exp(a_log) lies between 0.2 / 4096 and 0.5.
All inputs are finite; a program needn't handle non-finite values.
Results may differ from a plain program's by a relative error of at most 0.0049.
Values may be sent and summed in bfloat16 or wider, within the bound.
A program may use at most 128 MiB of HBM per device.

v0:
```python
import jax
import jax.numpy as jnp
from jax import lax
from jax.sharding import PartitionSpec as P

STATE = 256
BLOCK = 256
GROUP_DEVS = 4


exact_prec = lax.Precision.HIGHEST
norm_epsilon = 1e-05


def from_partner(array, axis, apart):
    return lax.ppermute(array, axis, [(i, i ^ 1 << apart) for i in range(lax.axis_size(axis))])


def group_total(values):
    bit_count = GROUP_DEVS.bit_length() - 1
    total = values
    for which_bit in range(bit_count):
        total = total + from_partner(total, "tensor", which_bit)
    return total


def group_share(stacked):
    bit_count = GROUP_DEVS.bit_length() - 1
    member = lax.axis_index("tensor") % GROUP_DEVS
    current = stacked
    for which_bit in reversed(range(bit_count)):
        half = current.shape[-1] // 2
        lower = current[..., :half]
        upper = current[..., half:]
        upper_side = member // (1 << which_bit) % 2 == 1
        keeping = jnp.where(upper_side, upper, lower)
        sending = jnp.where(upper_side, lower, upper)
        current = keeping + from_partner(sending, "tensor", which_bit)
    return current


def prepare_blocks(x_heads, b_rows, c_rows, dt_vals, dt_bias, a_rate, resets):
    length, heads, width = x_heads.shape
    count = length // BLOCK
    step = jax.nn.softplus(dt_vals + dt_bias[:, None])
    rate = step * a_rate[:, None]
    step_blocks = step.reshape(heads, count, BLOCK).transpose(1, 0, 2)
    rate_blocks = rate.reshape(heads, count, BLOCK).transpose(1, 0, 2)
    running = jnp.cumsum(rate_blocks, axis=2)
    segment = jnp.cumsum(resets.reshape(count, BLOCK), axis=1)
    x_blocks = x_heads.reshape(count, BLOCK, heads, width)
    b_blocks = b_rows.reshape(count, BLOCK, b_rows.shape[1])
    c_blocks = c_rows.reshape(count, BLOCK, c_rows.shape[1])
    places = jnp.arange(BLOCK)
    lower_tri = places[:, None] >= places[None, :]
    joined = ((segment[:, :, None] == segment[:, None, :]) & lower_tri[None])[:, None]
    spread = running[:, :, :, None] - running[:, :, None, :]
    weights = jnp.where(joined, jnp.exp(jnp.where(joined, spread, 0.0)), 0.0)
    scores = jnp.einsum("kin,kjn->kij", c_blocks, b_blocks, precision=exact_prec)
    mixing = weights * scores[:, None] * step_blocks[:, :, None, :]
    inside = jnp.einsum("khij,kjhp->kihp", mixing, x_blocks, precision=exact_prec)
    final_sum = running[:, :, -1:]
    closing = (segment == segment[:, -1:])[:, None]
    end_weight = (
        jnp.where(closing, jnp.exp(jnp.where(closing, final_sum - running, 0.0)), 0.0) * step_blocks
    )
    block_state = jnp.einsum(
        "khj,kjhp,kjn->khpn", end_weight, x_blocks, b_blocks, precision=exact_prec
    )
    block_keep = jnp.exp(final_sum[:, :, 0]) * (segment[:, -1] == 0).astype(jnp.float32)[:, None]
    opening = (segment == 0)[:, None]
    entry_decay = jnp.where(opening, jnp.exp(jnp.where(opening, running, 0.0)), 0.0)

    def advance(carry, item):
        keep_now, state_now = item
        keep_acc, state_acc = carry
        return ((keep_acc * keep_now, keep_now[:, None, None] * state_acc + state_now), carry)

    start_carry = (
        jnp.ones((heads,), jnp.float32),
        jnp.zeros((heads, width, b_rows.shape[1]), jnp.float32),
    )
    (whole_keep, whole_state), before = lax.scan(advance, start_carry, (block_keep, block_state))
    return (inside, entry_decay, before[0], before[1], whole_keep, whole_state)


def finish_blocks(
    inside, entry_decay, before_keep, before_state, c_rows, x_heads, gate_f, entering, skip_weight
):
    length, heads, width = x_heads.shape
    count = length // BLOCK
    c_blocks = c_rows.reshape(count, BLOCK, c_rows.shape[1])
    start_state = before_keep[:, :, None, None] * entering[None] + before_state
    carried = jnp.einsum(
        "khi,kin,khpn->kihp", entry_decay, c_blocks, start_state, precision=exact_prec
    )
    ssd_out = (inside + carried).reshape(length, heads, width) + skip_weight[
        None, :, None
    ] * x_heads
    return ssd_out.reshape(length, heads * width) * jax.nn.silu(gate_f)


def on_device(
    x_in,
    gate_in,
    b_in,
    c_in,
    dt_raw,
    dt_bias,
    a_log,
    skip_weight,
    norm_gain,
    w_out,
    doc_starts,
    grad_out,
):
    length = x_in.shape[0]
    heads = dt_raw.shape[0]
    width = x_in.shape[1] // heads
    ranks = lax.axis_size("context")
    my_rank = lax.axis_index("context")
    my_group = lax.axis_index("tensor") // GROUP_DEVS
    places = my_rank * length + jnp.arange(length, dtype=jnp.int32)
    resets = jnp.sum((places[:, None] == doc_starts[None, :]).astype(jnp.int32), axis=1)
    a_rate = -jnp.exp(a_log)
    x_heads = x_in.astype(jnp.float32).reshape(length, heads, width)
    gate_f = gate_in.astype(jnp.float32)
    column_start = my_group * STATE
    b_rows = lax.dynamic_slice_in_dim(b_in, column_start, STATE, 1).astype(jnp.float32)
    c_rows = lax.dynamic_slice_in_dim(c_in, column_start, STATE, 1).astype(jnp.float32)

    def prepare(x_vals, b_vals, c_vals, dt_vals):
        return prepare_blocks(x_vals, b_vals, c_vals, dt_vals, dt_bias, a_rate, resets)

    pieces, prepare_back = jax.vjp(prepare, x_heads, b_rows, c_rows, dt_raw)
    inside, entry_decay, before_keep, before_state, whole_keep, whole_state = pieces
    zero_state = jnp.zeros_like(whole_state)
    rank_list = jnp.arange(ranks, dtype=jnp.int32)
    keeps_all, states_all = (
        lax.all_gather(whole_keep[None], "context", axis=0, tiled=True),
        lax.all_gather(whole_state[None], "context", axis=0, tiled=True),
    )

    def fold_upward(acc, item):
        keep_one, state_one, rank_one = item
        return (jnp.where(rank_one < my_rank, keep_one[:, None, None] * acc + state_one, acc), None)

    entering, _ = lax.scan(fold_upward, zero_state, (keeps_all, states_all, rank_list))

    def finish(inside_v, entry_v, bkeep_v, bstate_v, c_vals, x_vals, gate_vals, enter_v):
        return finish_blocks(
            inside_v, entry_v, bkeep_v, bstate_v, c_vals, x_vals, gate_vals, enter_v, skip_weight
        )

    gated, finish_back = jax.vjp(
        finish, inside, entry_decay, before_keep, before_state, c_rows, x_heads, gate_f, entering
    )
    channels = GROUP_DEVS * gated.shape[1]
    factor = lax.rsqrt(group_total(jnp.sum(gated * gated, axis=1)) / channels + norm_epsilon)
    normed = gated * factor[:, None] * norm_gain[None, :]
    normed_half = normed.astype(jnp.bfloat16)
    mixed_out = lax.psum_scatter(
        jnp.dot(normed_half, w_out, preferred_element_type=jnp.float32),
        "tensor",
        scatter_dimension=0,
        tiled=True,
    ).astype(jnp.bfloat16)
    grad_normed = lax.dot_general(
        lax.all_gather(grad_out, "tensor", axis=0, tiled=True),
        w_out,
        (((1,), (1,)), ((), ())),
        preferred_element_type=jnp.float32,
    )
    scaled_grad = grad_normed * norm_gain[None, :]
    along = group_total(jnp.sum(scaled_grad * gated, axis=1))
    grad_gated = (
        scaled_grad * factor[:, None]
        - gated * (factor * factor * factor * along / channels)[:, None]
    )
    g_inside, g_entry, g_bkeep, g_bstate, g_c_late, g_x_late, g_gate, g_entering = finish_back(
        grad_gated
    )

    def spread_down(multiplier, item):
        keep_one, rank_one = item
        below = rank_one < my_rank
        result = jnp.where(below, multiplier, jnp.zeros_like(multiplier))
        return (jnp.where(below, multiplier * keep_one, multiplier), result)

    _, factors_all = lax.scan(
        spread_down, jnp.ones_like(whole_keep), (keeps_all, rank_list), reverse=True
    )
    terms_all = factors_all[:, :, None, None] * g_entering[None]
    later_grad = lax.psum_scatter(terms_all, "context", scatter_dimension=0, tiled=True)[0]
    g_whole_keep = jnp.sum(later_grad * entering, axis=(1, 2))
    g_x_early, g_b, g_c_early, g_dt = prepare_back(
        (g_inside, g_entry, g_bkeep, g_bstate, g_whole_keep, later_grad)
    )
    shares = group_share(jnp.stack([g_b, g_c_early + g_c_late]))
    grad_x = (g_x_early + g_x_late).reshape(length, heads * width).astype(jnp.bfloat16)
    grad_gate = g_gate.astype(jnp.bfloat16)
    grad_b = shares[0].astype(jnp.bfloat16)
    grad_c = shares[1].astype(jnp.bfloat16)
    return (mixed_out, grad_x, grad_gate, grad_b, grad_c, g_dt)


def solution(mesh):
    return jax.shard_map(
        on_device,
        mesh=mesh,
        in_specs=(
            P("context", "tensor"),
            P("context", "tensor"),
            P("context", None),
            P("context", None),
            P("tensor", "context"),
            P("tensor"),
            P("tensor"),
            P("tensor"),
            P("tensor"),
            P("tensor", None),
            P(),
            P(("context", "tensor"), None),
        ),
        out_specs=(
            P(("context", "tensor"), None),
            P("context", "tensor"),
            P("context", "tensor"),
            P("context", "tensor"),
            P("context", "tensor"),
            P("tensor", "context"),
        ),
        check_vma=False,
    )
```

profile of v0, /device:TPU:1, one launch (start us, length us, event | category | flops | bytes accessed | tf_op | source)
XLA Modules:
  0.0 355.1 jit_solution(401158254924008112)
XLA Ops:
  7.3 1.2 copy.78
  8.4 0.7 convert_reduce_fusion
  9.9 0.7 exponential_negate_fusion
  11.1 0.8 multiply_bitcast_fusion.1
  12.8 0.6 slice.61
  15.6 0.8 multiply_bitcast_fusion
  16.4 1.2 convolution_add_fusion
  17.7 0.7 all-gather.5.cloned.1.call-update
  18.7 17.1 %all-gather = f32[16,8,1]{1,2,0:T(1,128)S(1)} all-gather(f32[1,8,1]{1,2,0:T(1,128)S(1)} %copy.79), channel_id=2, replica_groups=mesh['context'=16,'tensor'=16] {'context'}, dimensions={0}, use_global_device_ids=true | all-gather | bytes 544 | tf_op jit(solution)/shard_map/all_gather | solution.py:140
  36.2 61.3 %all-gather.7.cloned.1.call-done = f32[128,64,256]{2,1,0:T(8,128)} async-done(((f32[8,64,256]{2,1,0:T(8,128)}), f32[128,64,256]{2,1,0:T(8,128)}) %all-gather.7.cloned.1.call-update) | async-done | bytes 8388624 | tf_op jit(solution)/shard_map/all_gather | solution.py:141
  97.5 39.3 %while.19 = (s32[]{:T(128)}, f32[8,64,256]{2,1,0:T(8,128)S(1)}, s32[16]{0:T(128)S(1)}, s32[]{:T(128)}, f32[16,8]{1,0:T(8,128)S(1)}, /*index=5*/f32[16,8,64,256]{3,2,1,0:T(8,128)}, s32[]{:T(128)}, s32[]{:T(128)}) while((s32[]{:T(128)}, f32[8,64,256]{2,1,0:T(8,128)S(1)}, s32[16]{0:T(128)S(1)}, s32[]{:T(128)}, f32[16,8]{1,0:T(8,128)S(1)}, ...), condition=%wide.region_6.7_spmd.clone, body=%wide.region_5.6_spmd.clone.sunk | while | flops 524292 | bytes 1573093 | solution.py:148
  98.7 1.2 fusion.118
  99.9 0.6 dynamic_slice.97
  101.2 1.2 fusion.118
  103.6 1.2 fusion.118
  104.8 0.6 dynamic_slice.97
  106.1 1.2 fusion.118
  107.3 0.6 dynamic_slice.97
  108.5 1.2 fusion.118
  109.8 0.6 dynamic_slice.97
  111.0 1.2 fusion.118
  112.2 0.6 dynamic_slice.97
  113.5 1.2 fusion.118
  114.7 0.6 dynamic_slice.97
  115.9 1.2 fusion.118
  117.1 0.6 dynamic_slice.97
  118.4 1.2 fusion.118
  120.8 1.2 fusion.118
  123.3 1.2 fusion.118
  125.8 1.2 fusion.118
  128.2 1.2 fusion.118
  130.7 1.2 fusion.118
  133.1 1.2 fusion.118
  135.6 1.2 fusion.118
  137.3 1.8 fusion.18
  139.3 2.5 all-gather.5.cloned.1.call-done
  141.8 7.8 %multiply_reduce_fusion.3 = (f32[256]{0:T(256)S(1)}, f32[256]{0:T(256)S(1)}, f32[256,512]{1,0:T(8,128)S(1)}, f32[256,512]{1,0:T(8,128)}) fusion(bf16[256,512]{1,0:T(8,128)(2,1)} %param.17, f32[256,512]{1,0:T(8,128)S(1)} %copy.82, bf16[256,512]{1,0:T(8,128)(2,1)S(1)} %copy-done.2, f32[512]{0:T(512)S(1)} %mul.347, f32[512]{0:T(512)S(1)} %copy-done.7, ...), kind=kOutput, calls=%fused_computation.72 | convolution fusion | flops 2149318144 | bytes 14686208 | tf_op jit(solution)/shard_map/dot_general | solution.py:168
  150.1 0.6 collective-permute-done.2
  150.8 0.8 collective-permute-start.3
  151.6 0.7 collective-permute-start.1
  152.2 21.1 %while.20 = (s32[]{:T(128)}, f32[8]{0:T(128)S(1)}, f32[16,8]{1,0:T(8,128)S(1)}, s32[16]{0:T(128)S(1)}, s32[]{:T(128)}, /*index=5*/f32[16,8]{1,0:T(8,128)S(1)}, s32[]{:T(128)}, s32[]{:T(128)}, s32[]{:T(128)}) while((s32[]{:T(128)}, f32[8]{0:T(128)S(1)}, f32[16,8]{1,0:T(8,128)S(1)}, s32[16]{0:T(128)S(1)}, s32[]{:T(128)}, ...), condition=%wide.region_10.11_spmd.clone, body=%wide.region_9.10_spmd.clone.sunk | while | flops 37 | bytes 345 | solution.py:190
  173.4 2.3 fusion.43
  175.8 1.3 fusion.45
  177.2 3.8 %broadcast_multiply_fusion = f32[16,8,64,256]{3,2,1,0:T(8,128)} fusion(f32[8,64,256]{2,1,0:T(8,128)S(1)} %fusion.45, f32[16,8]{1,0:T(8,128)S(1)} %get-tuple-element.218), kind=kLoop, calls=%fused_computation.7 | loop fusion | flops 2097152 | bytes 8913408 | tf_op jit(solution)/shard_map/mul | solution.py:193
  181.2 9.0 %fusion.54 = f32[256,8192]{1,0:T(8,128)} fusion(bf16[512,8192]{1,0:T(8,128)(2,1)} %param.25, f32[256,512]{1,0:T(8,128)S(1)} %get-tuple-element.361, f32[512]{0:T(512)S(1)} %copy-done.7, f32[256]{0:T(256)S(1)} %get-tuple-element.360), kind=kOutput, calls=%fused_computation.79 | convolution fusion | flops 2147876864 | bytes 17304576 | tf_op jit(solution)/shard_map/dot_general | solution.py:163
  190.3 0.9 copy-done.5
  191.2 3.3 fusion.24
  194.5 1.9 convolution_bitcast_fusion.3
  196.4 1.0 convolution_bitcast_fusion.2
  197.9 71.1 %reduce-scatter.7.cloned.1.call-done = f32[1,8,64,256]{3,2,1,0:T(8,128)} async-done(((f32[16,8,64,256]{3,2,1,0:T(8,128)}), f32[1,8,64,256]{3,2,1,0:T(8,128)}) %reduce-scatter.7.cloned.1.call-update) | async-done | bytes 524304
  269.0 2.2 fusion.22
  271.2 0.8 broadcast_select_fusion.3
  271.9 1.2 collective-permute-start.4
  273.1 1.3 fusion.37
  275.0 0.8 fusion.82
  275.9 2.5 reduce-window.26
  278.5 3.1 fusion.15
  281.8 57.8 %reduce-scatter.5.cloned.1.call-done = f32[16,8192]{1,0:T(8,128)} async-done(((f32[256,8192]{1,0:T(8,128)}), f32[16,8192]{1,0:T(8,128)}) %reduce-scatter.5.cloned.1.call-update) | async-done | bytes 524304 | tf_op jit(solution)/shard_map/reduce_scatter | solution.py:162
  339.6 1.8 convert_element_type.37
  341.4 0.8 add_convert_fusion
  342.2 1.0 select_add_fusion
  343.2 3.7 %collective-permute-start.5 = (f32[2,256,64]{1,2,0:T(8,128)S(1)}, f32[2,256,64]{1,2,0:T(8,128)S(1)}, u32[]{:S(2)}, u32[]{:S(2)}) collective-permute-start(f32[2,256,64]{1,2,0:T(8,128)S(1)} %slice_select_fusion), channel_id=1, source_target_pairs={{0,1},{1,0},{2,3},{3,2},{4,5},{5,4},{6,7},{7,6},{8,9},{9,8},{10,11... | collective-permute-start | bytes 393224 | tf_op jit(solution)/shard_map/ppermute | solution.py:16
  346.9 0.7 fusion.79
  348.0 0.6 slice_bitcast_fusion
  (161 shorter events, 22.9 us)
Async XLA Ops:
  7.2 9.3 %copy-start = (bf16[256,1024]{1,0:T(8,128)(2,1)S(1)}, bf16[256,1024]{1,0:T(8,128)(2,1)}, u32[]{:S(2)}) copy-start(bf16[256,1024]{1,0:T(8,128)(2,1)} %param.18) | copy-start | bytes 1572868
  7.2 11.4 %copy-start.13 = (f32[8]{0:T(128)S(1)}, f32[8]{0:T(128)}, u32[]{:S(2)}) copy-start(f32[8]{0:T(128)} %param.23) | copy-start | bytes 100
  7.2 28.7 %copy-start.3 = (bf16[256,1024]{1,0:T(8,128)(2,1)S(1)}, bf16[256,1024]{1,0:T(8,128)(2,1)}, u32[]{:S(2)}) copy-start(bf16[256,1024]{1,0:T(8,128)(2,1)} %param.19) | copy-start | bytes 1572868
  7.2 90.3 %all-gather.7.cloned.1.call-start = ((), (), s32[]{:S(2)}) async-start(), calls=%async_computation.4 | async-start | bytes 8912896 | tf_op jit(solution)/shard_map/all_gather | solution.py:141
  10.6 0.5 copy-start.11
  16.4 120.8 %copy-start.9 = (f32[8,256]{1,0:T(8,128)}, f32[8,256]{1,0:T(8,128)S(1)}, u32[]{:S(2)}) copy-start(f32[8,256]{1,0:T(8,128)S(1)} %get-tuple-element.373) | copy-start | bytes 24580
  17.7 124.1 %all-gather.5.cloned.1.call-start = ((), (), s32[]{:S(2)}) async-start(), calls=%async_computation.3 | async-start | bytes 4456448 | tf_op jit(solution)/shard_map/all_gather | solution.py:169
  18.4 250.5 %reduce-scatter.7.cloned.1.call-start = ((), (), s32[]{:S(2)}) async-start(), calls=%async_computation.5 | async-start | bytes 8912896
  36.1 101.2 %copy-start.4 = (f32[256,256]{1,0:T(8,128)}, f32[256,256]{1,0:T(8,128)S(1)}, u32[]{:S(2)}) copy-start(f32[256,256]{1,0:T(8,128)S(1)} %fusion.71) | copy-start | bytes 786436
  137.3 4.5 %copy-start.2 = (bf16[256,512]{1,0:T(8,128)(2,1)S(1)}, bf16[256,512]{1,0:T(8,128)(2,1)}, u32[]{:S(2)}) copy-start(bf16[256,512]{1,0:T(8,128)(2,1)} %param.16) | copy-start | bytes 786436
  137.3 4.5 %copy-start.7 = (f32[512]{0:T(512)S(1)}, f32[512]{0:T(512)}, u32[]{:S(2)}) copy-start(f32[512]{0:T(512)} %param.24) | copy-start | bytes 6148
  149.6 1.1 collective-permute-start.2
  149.9 1.7 collective-permute-start
  150.8 22.6 %collective-permute-start.3 = (f32[256]{0:T(256)S(1)}, f32[256]{0:T(256)S(1)}, u32[]{:S(2)}, u32[]{:S(2)}) collective-permute-start(f32[256]{0:T(256)S(1)} %add.141), channel_id=1, source_target_pairs={{0,2},{1,3},{2,0},{3,1},{4,6},{5,7},{6,4},{7,5},{8,10},{9,11},{10,... | collective-permute-start | bytes 3080 | tf_op jit(solution)/shard_map/ppermute | solution.py:16
  151.6 21.8 %collective-permute-start.1 = (f32[256]{0:T(256)S(1)}, f32[256]{0:T(256)S(1)}, u32[]{:S(2)}, u32[]{:S(2)}) collective-permute-start(f32[256]{0:T(256)S(1)} %add.137), channel_id=1, source_target_pairs={{0,2},{1,3},{2,0},{3,1},{4,6},{5,7},{6,4},{7,5},{8,10},{9,11},{10,... | collective-permute-start | bytes 3080 | tf_op jit(solution)/shard_map/ppermute | solution.py:16
  181.0 158.6 %reduce-scatter.5.cloned.1.call-start = ((), (), s32[]{:S(2)}) async-start(), calls=%async_computation.2 | async-start | bytes 8912896 | tf_op jit(solution)/shard_map/reduce_scatter | solution.py:162
  190.2 0.9 copy-start.5
  190.3 1.0 copy-start.10
  197.7 76.6 %copy-start.6 = (f32[8,256]{1,0:T(8,128)S(1)}, f32[8,256]{1,0:T(8,128)}, u32[]{:S(2)}) copy-start(f32[8,256]{1,0:T(8,128)} %param.20) | copy-start | bytes 24580
  197.8 76.6 %copy-start.8 = (f32[8]{0:T(128)S(1)}, f32[8]{0:T(128)}, u32[]{:S(2)}) copy-start(f32[8]{0:T(128)} %param.21) | copy-start | bytes 100
  269.0 4.1 %copy-start.1 = (f32[1,8,64,256]{3,2,1,0:T(8,128)S(1)}, f32[1,8,64,256]{3,2,1,0:T(8,128)}, u32[]{:S(2)}) copy-start(f32[1,8,64,256]{3,2,1,0:T(8,128)} %reduce-scatter.7.cloned.1.call-done) | copy-start | bytes 1572868
  271.9 70.3 %collective-permute-start.4 = (f32[2,256,128]{1,2,0:T(8,128)}, f32[2,256,128]{1,2,0:T(8,128)}, u32[]{:S(2)}, u32[]{:S(2)}) collective-permute-start(f32[2,256,128]{1,2,0:T(8,128)} %broadcast_select_fusion.3), channel_id=1, source_target_pairs={{0,2},{1,3},{2,0},{3,1},{4,6},{5,7},{6,4},{7,5},{8,10},{9,11},{10,... | collective-permute-start | bytes 786440 | tf_op jit(solution)/shard_map/ppermute | solution.py:16
  281.6 65.3 %copy-start.12 = (f32[8]{0:T(128)S(1)}, f32[8]{0:T(128)}, u32[]{:S(2)}) copy-start(f32[8]{0:T(128)} %copy-done.11) | copy-start | bytes 100
  343.2 4.7 %collective-permute-start.5 = (f32[2,256,64]{1,2,0:T(8,128)S(1)}, f32[2,256,64]{1,2,0:T(8,128)S(1)}, u32[]{:S(2)}, u32[]{:S(2)}) collective-permute-start(f32[2,256,64]{1,2,0:T(8,128)S(1)} %slice_select_fusion), channel_id=1, source_target_pairs={{0,1},{1,0},{2,3},{3,2},{4,5},{5,4},{6,7},{7,6},{8,9},{9,8},{10,11... | collective-permute-start | bytes 393224 | tf_op jit(solution)/shard_map/ppermute | solution.py:16
Sparse Core Ops, SparseCore 0:
  17.8 79.6 all-gather.6
  99.3 42.4 all-gather.4
  181.1 87.8 reduce-scatter.6
  271.4 68.1 reduce-scatter.4
where the time goes:
time: 357 us; the launch traced here: 355 us
  waiting for transfers between devices  194 us (54%)
  other arithmetic  38.9 us (11%)
  matrix products  34.9 us (10%)
  local copies, waits for them, and re-layouts  25.4 us (7%)
  loops' own time  21.7 us (6%)
  blocking collectives  17.1 us (5%)
  between operations  15.5 us (4%)
  starting transfers between devices  7.22 us (2%)
    unnamed x5, waiting for transfers between devices  71.9 us
    all_gather x1, waiting for transfers between devices, on_device(): lax.all_gather(whole_state[None], 'context', axis=0, tiled=True)  61.3 us
    reduce_scatter x1, waiting for transfers between devices, on_device(): lax.psum_scatter(jnp.dot(normed_half, w_out, preferred_element_type=jnp.f...  57.8 us
    select_n x16, other arithmetic, fold_upward(): jnp.where(rank_one < my_rank, keep_one[:, None, None] * acc + state_one,...  18.9 us
    dynamic_slice x32, local copies, waits for them, and re-layouts, on_device(): lax.scan(fold_upward, zero_state, (keeps_all, states_all, rank_list))  18.8 us
    all_gather x1, blocking collectives, on_device(): lax.all_gather(whole_keep[None], 'context', axis=0, tiled=True)  17.1 us
    another operation x1, loops' own time, on_device(): lax.scan(fold_upward, zero_state, (keeps_all, states_all, rank_list))  10.9 us
    another operation x1, loops' own time, on_device(): lax.scan(spread_down, jnp.ones_like(whole_keep), (keeps_all, rank_list),...  10.8 us
  transfers between devices with their start and end apart: 10, of which 6 were waited for; matrix products, arithmetic and copies ran while one was open for 20% of the time, Pallas kernels for 0%

commit v1 on v0

v1 whole, which is shorter than its diff:
```python
import jax
import jax.numpy as jnp
from jax import lax
from jax.experimental import pallas as pl
from jax.experimental.pallas import tpu as pltpu
from jax.sharding import PartitionSpec as P

F32 = jnp.float32
BF16 = jnp.bfloat16
HIGH = lax.Precision.HIGHEST
RANKS = 16
SHARDS = 16
RING = 8
HEADS = 8
WIDTH = 64
CHANNELS = HEADS * WIDTH
STATE = 256
ROWS = 256
MODEL = 8192
HALF = MODEL // 2
CHIP_ROWS = ROWS // RING
OWN_ROWS = CHIP_ROWS // 2
PIECE = HALF // 2
CHUNK = CHANNELS // RANKS
GROUP_CHANNELS = 2048
EPS = 1e-05


def nn(a, b, precision=None):
    return lax.dot_general(
        a, b, (((1,), (0,)), ((), ())), preferred_element_type=F32, precision=precision
    )


def nt(a, b):
    return lax.dot_general(a, b, (((1,), (1,)), ((), ())), preferred_element_type=F32)


def tn(a, b):
    return lax.dot_general(a, b, (((0,), (0,)), ((), ())), preferred_element_type=F32)


def streams(way, hop):
    if way == 0:
        return (0, 1) if hop else (0,)
    return (1, 0) if hop else (1,)


def layer(
    x_ref,
    gate_ref,
    b_hbm,
    c_hbm,
    dt_ref,
    bias_ref,
    alog_ref,
    skip_ref,
    gain_ref,
    w_hbm,
    docs_ref,
    go_hbm,
    mixed_ref,
    gx_ref,
    gg_ref,
    gbc_ref,
    gdt_ref,
    bv,
    cv,
    wv,
    gbuf,
    xt,
    r_s,
    e_s,
    wend_s,
    step_s,
    qcol,
    mask,
    gt,
    ws,
    mt,
    yin,
    car,
    yt,
    gated,
    sl,
    dsl,
    gcol,
    wxt,
    wxn,
    fsum,
    keep,
    sb,
    rb,
    eb,
    s0,
    sb2,
    rb2,
    eb2,
    zz,
    gn,
    nbuf,
    abuf,
    fc,
    pp,
    rsend,
    rrecv,
    qsend,
    qrecv,
    dyb,
    edy,
    dgt,
    dxin,
    rowdot,
    coldot,
    cardot,
    zdot,
    gown,
    gsend,
    grecv,
    ob,
    orecv,
    loc,
    pair_s,
    pair_r,
    ag_s,
    ag_r,
    rs_s,
    rs_r,
    ex_s,
    ex_r,
    gr_s,
    gr_r,
):
    rank = lax.axis_index("context")
    shard = lax.axis_index("tensor")
    chip = shard // 2
    core = shard % 2
    other = 1 - core
    group = shard // 4
    member = shard % 4
    sibling = chip * 2 + other
    ahead = ((chip + 1) % RING) * 2 + core
    behind = ((chip + RING - 1) % RING) * 2 + core
    mates = (None, 1 + member - 2 * (member % 2), (member + 2) % 4, 3 - member)

    def remote(src, dst, send, recv, c_to, t_to):
        return pltpu.make_async_remote_copy(
            src_ref=src,
            dst_ref=dst,
            send_sem=send,
            recv_sem=recv,
            device_id=(c_to, t_to),
            device_id_type=pl.DeviceIdType.MESH,
        )

    def each(first, last, body):
        def step(i, carry):
            body(i)
            return carry

        lax.fori_loop(first, last, step, 0)

    barrier = pltpu.get_barrier_semaphore()

    def greet(c_to, t_to):
        pl.semaphore_signal(
            barrier, inc=1, device_id=(c_to, t_to), device_id_type=pl.DeviceIdType.MESH
        )

    greet(rank, sibling)
    greet(rank, group * 4 + mates[3])
    greet(rank, ahead)
    greet(rank, behind)
    each(1, RANKS, lambda k: greet((rank + k) % RANKS, shard))

    here = pl.ds(pl.multiple_of(core * HALF, HALF), HALF)
    there = pl.ds(pl.multiple_of(other * HALF, HALF), HALF)
    mine = pl.ds(pl.multiple_of(core * OWN_ROWS, OWN_ROWS), OWN_ROWS)
    columns = pl.ds(pl.multiple_of(group * STATE, STATE), STATE)
    load_go = pltpu.make_async_copy(go_hbm.at[:, here], gbuf.at[chip, mine, :], loc.at[0])
    load_b = pltpu.make_async_copy(b_hbm.at[:, columns], bv, loc.at[1])
    load_c = pltpu.make_async_copy(c_hbm.at[:, columns], cv, loc.at[2])
    load_w = pltpu.make_async_copy(w_hbm.at[:, here], wv.at[core], loc.at[3])
    load_go.start()
    load_b.start()
    load_c.start()
    load_w.start()

    head_rows = lax.broadcasted_iota(jnp.int32, (HEADS, ROWS), 0)

    def per_head(ref):
        total = jnp.zeros((HEADS, ROWS), F32)
        for h in range(HEADS):
            total = jnp.where(head_rows == h, ref[h], total)
        return total

    raw = dt_ref[...] + per_head(bias_ref)
    a_rate = -jnp.exp(per_head(alog_ref))
    step = jnp.maximum(raw, 0.0) + jnp.log1p(jnp.exp(-jnp.abs(raw)))
    row_ids = lax.broadcasted_iota(jnp.int32, (ROWS, ROWS), 0)
    col_ids = lax.broadcasted_iota(jnp.int32, (ROWS, ROWS), 1)
    upto = jnp.where(row_ids <= col_ids, 1.0, 0.0)
    running = nn(step * a_rate, upto, HIGH)
    final = running[:, ROWS - 1 : ROWS]
    base = rank * ROWS
    starts = []
    for i in range(4):
        begin = docs_ref[i]
        starts.append(jnp.where(begin >= base, begin - base, 1 << 20))
    pos_row = lax.broadcasted_iota(jnp.int32, (1, ROWS), 1)
    pos_col = lax.broadcasted_iota(jnp.int32, (ROWS, 1), 0)
    seg_row = jnp.zeros((1, ROWS), jnp.int32)
    seg_col = jnp.zeros((ROWS, 1), jnp.int32)
    seg_last = jnp.int32(0)
    for begin in starts:
        seg_row = seg_row + jnp.where(pos_row >= begin, 1, 0)
        seg_col = seg_col + jnp.where(pos_col >= begin, 1, 0)
        seg_last = seg_last + jnp.where(begin <= ROWS - 1, 1, 0)
    opening = seg_row == 0
    closing = seg_row == seg_last
    r_s[...] = running
    step_s[...] = step
    e_s[...] = jnp.where(opening, jnp.exp(running), 0.0)
    wend_s[...] = jnp.where(closing, jnp.exp(final - running), 0.0) * step
    mask[...] = jnp.where((seg_col == seg_row) & (row_ids <= col_ids), 0.0, -1e30)
    shifted = (running - jnp.log(step)).T
    for h in range(HEADS):
        qcol[h] = jnp.broadcast_to(shifted[:, h : h + 1], (ROWS, 128))
    fsum[rank] = jnp.broadcast_to(final, (HEADS, 128))
    xt[...] = x_ref[...].T.reshape(HEADS, WIDTH, ROWS)

    pl.semaphore_wait(barrier, 4 + RANKS - 1)
    pair_go = remote(
        go_hbm.at[:, there], gbuf.at[chip, mine, :], pair_s.at[0], pair_r.at[0], rank, sibling
    )
    pair_w = remote(w_hbm.at[:, there], wv.at[core], pair_s.at[1], pair_r.at[1], rank, sibling)
    pair_go.start()
    pair_w.start()

    def spread(which, src, dst, own_src):
        def copy(k):
            to = (rank + k) % RANKS
            return remote(
                src.at[rank] if own_src else src.at[to],
                dst.at[rank],
                ex_s.at[which, k],
                ex_r.at[which, k],
                to,
                shard,
            )

        return copy

    ex_keep = spread(0, fsum, fsum, True)
    ex_state = spread(1, sb, rb, False)
    ex_enter = spread(2, eb, s0, False)
    ex_grad = spread(3, sb2, rb2, False)
    ex_later = spread(4, eb2, zz, False)
    each(1, RANKS, lambda k: ex_keep(k).start())

    def ag_copy(hop, way, piece):
        block = (chip + RING - hop) % RING if way == 0 else (chip + hop) % RING
        cols = pl.ds(piece * PIECE, PIECE)
        slot = (hop * 2 + way) * 2 + piece
        return remote(
            gbuf.at[block, :, cols],
            gbuf.at[block, :, cols],
            ag_s.at[slot],
            ag_r.at[slot],
            rank,
            ahead if way == 0 else behind,
        )

    def ag_streams(way, hop):
        return streams(way, 3 - hop)

    def ag_hop(hop):
        for way in range(2):
            for piece in ag_streams(way, hop):
                if hop:
                    ag_copy(hop - 1, way, piece).wait_recv()
                ag_copy(hop, way, piece).start()

    load_go.wait()
    pair_go.wait_recv()
    ag_hop(0)

    load_b.wait()
    load_c.wait()
    for h in range(HEADS):
        wxt[h] = wend_s[h : h + 1, :] * xt[h].astype(F32)
    wx_all = wxt[...].reshape(CHANNELS, ROWS)
    wx_hi = wx_all.astype(BF16)
    wx_lo = (wx_all - wx_hi.astype(F32)).astype(BF16)
    end_state = nn(wx_hi, bv[...]) + nn(wx_lo, bv[...])
    sb[...] = end_state.astype(BF16).reshape(RANKS, CHUNK, STATE)
    each(1, RANKS, lambda k: ex_state(k).start())
    rb[rank] = sb[rank]
    wxn[...] = wx_hi.T

    gt[...] = nt(bv[...], cv[...])

    def inside(h):
        q = qcol[h]
        weight = jnp.exp(r_s[pl.ds(h, 1), :] - jnp.concatenate([q, q], axis=1) + mask[...])
        ws[h] = weight
        mixing = (weight * gt[...]).astype(BF16)
        mt[h] = mixing
        yin[h] = nn(xt[h], mixing)

    each(0, HEADS, inside)
    ag_hop(1)

    each(1, RANKS, lambda k: ex_keep(k).wait_recv())
    for r in range(RANKS):
        count = jnp.int32(0)
        for i in range(4):
            begin = docs_ref[i]
            count = count + jnp.where((begin >= r * ROWS) & (begin < (r + 1) * ROWS), 1, 0)
        whole = jnp.where(count == 0, 1.0, 0.0)
        keep[r] = jnp.exp(fsum[r]) * whole
    my_head = rank // 2

    def keep_of(r):
        row = keep[r, pl.ds(my_head, 1), :]
        return jnp.concatenate([row, row], axis=1)

    each(1, RANKS, lambda k: ex_state(k).wait_recv())
    total = jnp.zeros((CHUNK, STATE), F32)
    for r in range(RANKS):
        eb[r] = total.astype(BF16)
        total = keep_of(r) * total + rb[r].astype(F32)
    each(1, RANKS, lambda k: ex_enter(k).start())
    s0[rank] = eb[rank]

    v = gate_ref[...].T.astype(F32)
    sig = 1.0 / (1.0 + jnp.exp(-v))
    sl[...] = (v * sig).reshape(HEADS, WIDTH, ROWS)
    dsl[...] = (sig * (1.0 + v * (1.0 - sig))).reshape(HEADS, WIDTH, ROWS)
    eye = row_ids == col_ids
    for q in range(CHANNELS // 128):
        line = gain_ref[:, q * 128 : (q + 1) * 128]
        picked = jnp.where(eye[:128, :128], line, 0.0)
        column = jnp.sum(picked, axis=1, keepdims=True)
        gcol[2 * q : 2 * q + 2] = jnp.broadcast_to(column, (128, 128)).reshape(2, WIDTH, 128)
    ag_hop(2)

    each(1, RANKS, lambda k: ex_enter(k).wait_recv())
    enter_all = s0[...].reshape(CHANNELS, STATE)
    car[...] = nt(enter_all, cv[...]).reshape(HEADS, WIDTH, ROWS)

    def finish(h, squares):
        moved = e_s[pl.ds(h, 1), :] * car[h]
        car[h] = moved
        out = yin[h] + moved + skip_ref[h] * xt[h].astype(F32)
        yt[h] = out
        value = out * sl[h]
        gated[h] = value
        return squares + jnp.sum(value * value, axis=0, keepdims=True)

    squares = lax.fori_loop(0, HEADS, finish, jnp.zeros((1, ROWS), F32))
    nbuf[0] = squares

    def mate_copy(which, buf, x):
        return remote(
            buf.at[0],
            buf.at[x],
            gr_s.at[which, x],
            gr_r.at[which, x],
            rank,
            group * 4 + mates[x],
        )

    for x in (1, 2, 3):
        mate_copy(0, nbuf, x).start()
    gain_full = jnp.concatenate([gcol[...], gcol[...]], axis=2)
    scaled = (gated[...] * gain_full).reshape(CHANNELS, ROWS).astype(BF16)
    gn[core] = scaled.T
    pair_gn = remote(gn.at[core], gn.at[core], pair_s.at[2], pair_r.at[2], rank, sibling)
    pair_gn.start()
    ag_hop(3)

    load_w.wait()
    pair_w.wait_recv()
    pair_gn.wait_recv()
    tile = 512

    def product(n):
        cols = pl.ds(pl.multiple_of(n * tile, tile), tile)
        value = nn(gn[0], wv[0, :, cols]) + nn(gn[1], wv[1, :, cols])
        pp[:, :, cols] = value.reshape(RING, CHIP_ROWS, tile)

    each(0, HALF // tile, product)
    for x in (1, 2, 3):
        mate_copy(0, nbuf, x).wait_recv()
    mean = (nbuf[0] + nbuf[1] + nbuf[2] + nbuf[3]) * (1.0 / GROUP_CHANNELS)
    factor = lax.rsqrt(mean + EPS)
    factor_col = jnp.sum(jnp.where(eye, factor, 0.0), axis=1, keepdims=True)
    fc[...] = jnp.broadcast_to(factor_col, (ROWS, 128)).reshape(RING, CHIP_ROWS, 128)

    def own_part(block, piece):
        lanes = fc[block]
        return pp[block, :, piece * PIECE : (piece + 1) * PIECE] * jnp.concatenate(
            [lanes] * (PIECE // 128), axis=1
        )

    def rs_copy(hop, way, piece):
        cols = pl.ds(piece * PIECE, PIECE)
        slot = (hop * 2 + way) * 2 + piece
        return remote(
            rsend.at[way, hop, :, cols],
            rrecv.at[way, hop, :, cols],
            rs_s.at[slot],
            rs_r.at[slot],
            rank,
            ahead if way == 0 else behind,
        )

    def rs_hop(hop):
        for way in range(2):
            block = (chip + 4 - hop) % RING if way == 0 else (chip + 4 + hop) % RING
            for piece in streams(way, hop):
                cols = pl.ds(piece * PIECE, PIECE)
                value = own_part(block, piece)
                if hop and piece in streams(way, hop - 1):
                    rs_copy(hop - 1, way, piece).wait_recv()
                    value = value + rrecv[way, hop - 1, :, cols].astype(F32)
                rsend[way, hop, :, cols] = value.astype(BF16)
                rs_copy(hop, way, piece).start()

    rs_hop(0)

    for way in range(2):
        for piece in range(2):
            hop = 3 if piece in ag_streams(way, 3) else 2
            ag_copy(hop, way, piece).wait_recv()
    cotangent = gbuf[...].reshape(ROWS, HALF)
    qsend[...] = nt(wv[other], cotangent)
    pair_q = remote(qsend, qrecv, pair_s.at[3], pair_r.at[3], rank, sibling)
    pair_q.start()
    grad_own = nt(wv[core], cotangent)
    rs_hop(1)
    pair_q.wait_recv()
    grad_scaled = (grad_own + qrecv[...]).reshape(HEADS, WIDTH, ROWS) * gain_full
    along = jnp.sum(
        (grad_scaled * gated[...]).reshape(CHANNELS, ROWS), axis=0, keepdims=True
    )
    abuf[0] = along
    for x in (1, 2, 3):
        mate_copy(1, abuf, x).start()
    for x in (1, 2, 3):
        mate_copy(1, abuf, x).wait_recv()
    along = abuf[0] + abuf[1] + abuf[2] + abuf[3]
    bend = factor * factor * factor * along * (1.0 / GROUP_CHANNELS)
    grad_gated = grad_scaled * factor[None] - gated[...] * bend[None]
    dy_all = grad_gated * sl[...]
    dyb[...] = dy_all.astype(BF16)
    grad_gate = (grad_gated * yt[...] * dsl[...]).astype(BF16)
    gg_ref[...] = grad_gate.reshape(CHANNELS, ROWS).T

    for h in range(HEADS):
        edy[h] = (e_s[h : h + 1, :] * dyb[h].astype(F32)).astype(BF16)
    edy_all = edy[...].reshape(CHANNELS, ROWS)
    sb2[...] = nn(edy_all, cv[...]).astype(BF16).reshape(RANKS, CHUNK, STATE)
    each(1, RANKS, lambda k: ex_grad(k).start())
    rb2[rank] = sb2[rank]

    dgt[...] = jnp.zeros((ROWS, ROWS), F32)

    def back(h):
        dy = dyb[h]
        x_now = xt[h]
        dgt[...] += ws[h] * tn(x_now, dy)
        grad_in = nt(dy, mt[h])
        dxin[h] = grad_in
        dyf = dy.astype(F32)
        rowdot[pl.ds(h, 1), :] = jnp.sum(dyf * yin[h], axis=0, keepdims=True)
        cardot[pl.ds(h, 1), :] = jnp.sum(dyf * car[h], axis=0, keepdims=True)
        coldot[pl.ds(h, 1), :] = jnp.sum(x_now.astype(F32) * grad_in, axis=0, keepdims=True)

    each(0, HEADS, back)
    rs_hop(2)

    each(1, RANKS, lambda k: ex_grad(k).wait_recv())
    total = jnp.zeros((CHUNK, STATE), F32)
    for r in reversed(range(RANKS)):
        eb2[r] = total.astype(BF16)
        total = keep_of(r) * total + rb2[r].astype(F32)
    each(1, RANKS, lambda k: ex_later(k).start())
    zz[rank] = eb2[rank]

    grad_scores = dgt[...].astype(BF16)
    grad_c = tn(grad_scores, bv[...]) + nn(edy_all.T, enter_all)
    grad_b = nn(grad_scores, cv[...])
    rs_hop(3)

    each(1, RANKS, lambda k: ex_later(k).wait_recv())
    later = zz[...].reshape(CHANNELS, STATE)
    grad_b = grad_b + nn(wxn[...], later)
    lane = lax.broadcasted_iota(jnp.int32, (ROWS, 128), 1)
    for q in range(2):
        tile_b = grad_b[:, q * 128 : (q + 1) * 128]
        tile_c = grad_c[:, q * 128 : (q + 1) * 128]
        gown[2 * q] = jnp.where(lane < 64, tile_b, pltpu.roll(tile_c, 64, 1))
        gown[2 * q + 1] = jnp.where(lane < 64, pltpu.roll(tile_b, 64, 1), tile_c)
    gsend[...] = gown[...].astype(BF16)

    def share_copy(x):
        return remote(
            gsend.at[mates[x]],
            grecv.at[x],
            gr_s.at[2, x],
            gr_r.at[2, x],
            rank,
            group * 4 + mates[x],
        )

    for x in (1, 2, 3):
        share_copy(x).start()

    moved_back = nt(later, bv[...])
    inner = jnp.zeros((HEADS, ROWS), F32)
    overlap = later.astype(F32) * enter_all.astype(F32)
    for h in range(HEADS):
        part = moved_back[h * WIDTH : (h + 1) * WIDTH, :]
        part = wend_s[h : h + 1, :] * part
        x_now = xt[h].astype(F32)
        zdot[h : h + 1, :] = jnp.sum(x_now * part, axis=0, keepdims=True)
        dxin[h] = dxin[h] + part + skip_ref[h] * dyb[h].astype(F32)
        block = overlap[h * WIDTH : (h + 1) * WIDTH, :]
        inner = jnp.where(head_rows == h, jnp.sum(block), inner)
    gx_ref[...] = dxin[...].reshape(CHANNELS, ROWS).astype(BF16).T

    from_here = jnp.where(row_ids >= col_ids, 1.0, 0.0)
    before = jnp.where(row_ids < col_ids, 1.0, 0.0)
    kept = jnp.where(seg_last == 0, 1.0, 0.0) * jnp.exp(final)
    grad_rate = (
        nn(rowdot[...] - coldot[...] + cardot[...], from_here, HIGH)
        + nn(zdot[...], before, HIGH)
        + kept * inner
    )
    grad_step = (coldot[...] + zdot[...]) / step_s[...] + a_rate * grad_rate
    gdt_ref[...] = grad_step * (1.0 / (1.0 + jnp.exp(-raw)))

    for way in range(2):
        for piece in range(2):
            rs_copy(3, way, piece).wait_recv()
    for piece in range(2):
        cols = pl.ds(piece * PIECE, PIECE)
        value = (
            own_part(chip, piece)
            + rrecv[0, 3, :, cols].astype(F32)
            + rrecv[1, 3, :, cols].astype(F32)
        )
        ob[:, :, cols] = value.astype(BF16).reshape(2, OWN_ROWS, PIECE)
    pair_out = remote(ob.at[other], orecv, pair_s.at[4], pair_r.at[4], rank, sibling)
    pair_out.start()
    mixed_ref[:, here] = ob[core]
    for x in (1, 2, 3):
        share_copy(x).wait_recv()
    shares = gown[member]
    for x in (1, 2, 3):
        shares = shares + grecv[x].astype(F32)
    gbc_ref[...] = shares.astype(BF16)
    pair_out.wait_recv()
    mixed_ref[:, there] = orecv[...]

    for copy in (pair_go, pair_w, pair_gn, pair_q, pair_out):
        copy.wait_send()
    for hop in range(4):
        for way in range(2):
            for piece in ag_streams(way, hop):
                ag_copy(hop, way, piece).wait_send()
            for piece in streams(way, hop):
                rs_copy(hop, way, piece).wait_send()
    for exchange in (ex_keep, ex_state, ex_enter, ex_grad, ex_later):
        each(1, RANKS, lambda k: exchange(k).wait_send())
    for x in (1, 2, 3):
        mate_copy(0, nbuf, x).wait_send()
        mate_copy(1, abuf, x).wait_send()
        share_copy(x).wait_send()


def on_device(
    x_in,
    gate_in,
    b_in,
    c_in,
    dt_raw,
    dt_bias,
    a_log,
    skip_weight,
    norm_gain,
    w_out,
    doc_starts,
    grad_out,
):
    vmem = pl.BlockSpec(memory_space=pltpu.VMEM)
    smem = pl.BlockSpec(memory_space=pltpu.SMEM)
    anywhere = pl.BlockSpec(memory_space=pl.ANY)
    by_head = (HEADS, WIDTH, ROWS)
    by_rank = (RANKS, CHUNK, STATE)
    dma = pltpu.SemaphoreType.DMA
    out = pl.pallas_call(
        layer,
        out_shape=[
            jax.ShapeDtypeStruct((OWN_ROWS, MODEL), BF16),
            jax.ShapeDtypeStruct((ROWS, CHANNELS), BF16),
            jax.ShapeDtypeStruct((ROWS, CHANNELS), BF16),
            jax.ShapeDtypeStruct((ROWS, 128), BF16),
            jax.ShapeDtypeStruct((HEADS, ROWS), F32),
        ],
        in_specs=[
            vmem,
            vmem,
            anywhere,
            anywhere,
            vmem,
            smem,
            smem,
            smem,
            vmem,
            anywhere,
            smem,
            anywhere,
        ],
        out_specs=[vmem] * 5,
        scratch_shapes=[
            pltpu.VMEM((ROWS, STATE), BF16),
            pltpu.VMEM((ROWS, STATE), BF16),
            pltpu.VMEM((2, CHANNELS, HALF), BF16),
            pltpu.VMEM((RING, CHIP_ROWS, HALF), BF16),
            pltpu.VMEM(by_head, BF16),
            pltpu.VMEM((HEADS, ROWS), F32),
            pltpu.VMEM((HEADS, ROWS), F32),
            pltpu.VMEM((HEADS, ROWS), F32),
            pltpu.VMEM((HEADS, ROWS), F32),
            pltpu.VMEM((HEADS, ROWS, 128), F32),
            pltpu.VMEM((ROWS, ROWS), F32),
            pltpu.VMEM((ROWS, ROWS), F32),
            pltpu.VMEM((HEADS, ROWS, ROWS), F32),
            pltpu.VMEM((HEADS, ROWS, ROWS), BF16),
            pltpu.VMEM(by_head, F32),
            pltpu.VMEM(by_head, F32),
            pltpu.VMEM(by_head, F32),
            pltpu.VMEM(by_head, F32),
            pltpu.VMEM(by_head, F32),
            pltpu.VMEM(by_head, F32),
            pltpu.VMEM((HEADS, WIDTH, 128), F32),
            pltpu.VMEM(by_head, F32),
            pltpu.VMEM((ROWS, CHANNELS), BF16),
            pltpu.VMEM((RANKS, HEADS, 128), F32),
            pltpu.VMEM((RANKS, HEADS, 128), F32),
            pltpu.VMEM(by_rank, BF16),
            pltpu.VMEM(by_rank, BF16),
            pltpu.VMEM(by_rank, BF16),
            pltpu.VMEM(by_rank, BF16),
            pltpu.VMEM(by_rank, BF16),
            pltpu.VMEM(by_rank, BF16),
            pltpu.VMEM(by_rank, BF16),
            pltpu.VMEM(by_rank, BF16),
            pltpu.VMEM((2, ROWS, CHANNELS), BF16),
            pltpu.VMEM((4, 1, ROWS), F32),
            pltpu.VMEM((4, 1, ROWS), F32),
            pltpu.VMEM((RING, CHIP_ROWS, 128), F32),
            pltpu.VMEM((RING, CHIP_ROWS, HALF), F32),
            pltpu.VMEM((2, 4, CHIP_ROWS, HALF), BF16),
            pltpu.VMEM((2, 4, CHIP_ROWS, HALF), BF16),
            pltpu.VMEM((CHANNELS, ROWS), F32),
            pltpu.VMEM((CHANNELS, ROWS), F32),
            pltpu.VMEM(by_head, BF16),
            pltpu.VMEM(by_head, BF16),
            pltpu.VMEM((ROWS, ROWS), F32),
            pltpu.VMEM(by_head, F32),
            pltpu.VMEM((HEADS, ROWS), F32),
            pltpu.VMEM((HEADS, ROWS), F32),
            pltpu.VMEM((HEADS, ROWS), F32),
            pltpu.VMEM((HEADS, ROWS), F32),
            pltpu.VMEM((4, ROWS, 128), F32),
            pltpu.VMEM((4, ROWS, 128), BF16),
            pltpu.VMEM((4, ROWS, 128), BF16),
            pltpu.VMEM((2, OWN_ROWS, HALF), BF16),
            pltpu.VMEM((OWN_ROWS, HALF), BF16),
            dma((4,)),
            dma((5,)),
            dma((5,)),
            dma((16,)),
            dma((16,)),
            dma((16,)),
            dma((16,)),
            dma((5, RANKS)),
            dma((5, RANKS)),
            dma((3, 4)),
            dma((3, 4)),
        ],
        compiler_params=pltpu.CompilerParams(
            collective_id=0, has_side_effects=True, vmem_limit_bytes=56 * 1024 * 1024
        ),
        cost_estimate=pl.CostEstimate(
            flops=6_000_000_000, bytes_accessed=16_000_000, transcendentals=1_000_000
        ),
        name="layer",
    )(
        x_in,
        gate_in,
        b_in,
        c_in,
        dt_raw,
        dt_bias,
        a_log,
        skip_weight,
        norm_gain.reshape(1, CHANNELS),
        w_out,
        doc_starts,
        grad_out,
    )
    mixed, grad_x, grad_gate, grad_bc, grad_dt = out
    return (mixed, grad_x, grad_gate, grad_bc[:, :64], grad_bc[:, 64:], grad_dt)


def solution(mesh):
    return jax.shard_map(
        on_device,
        mesh=mesh,
        in_specs=(
            P("context", "tensor"),
            P("context", "tensor"),
            P("context", None),
            P("context", None),
            P("tensor", "context"),
            P("tensor"),
            P("tensor"),
            P("tensor"),
            P("tensor"),
            P("tensor", None),
            P(),
            P(("context", "tensor"), None),
        ),
        out_specs=(
            P(("context", "tensor"), None),
            P("context", "tensor"),
            P("context", "tensor"),
            P("context", "tensor"),
            P("context", "tensor"),
            P("tensor", "context"),
        ),
        check_vma=False,
    )
```

time: 357 us -> 81.1 us (0.23)
  waiting for transfers between devices: 194 us -> 0 us
  Pallas kernels: 0 us -> 71.5 us
  other arithmetic: 38.9 us -> 0 us
  matrix products: 34.9 us -> 0 us
  loops' own time: 21.7 us -> 0 us
  blocking collectives: 17.1 us -> 0 us
  local copies, waits for them, and re-layouts: 25.4 us -> 8.72 us
  between operations: 15.5 us -> 0.65 us
  starting transfers between devices: 7.22 us -> 0 us
    unnamed x5 -> x0, waiting for transfers between devices: 71.9 us -> none
    pallas_call x0 -> x1, Pallas kernels: none -> 71.5 us  [on_device(): pl.pallas_call(layer, out_shape=[jax.ShapeDtypeStruct((OWN_ROWS, MODEL),...]
    all_gather x2 -> x0, waiting for transfers between devices: 63.8 us -> none  [the longest x1 61.3 us: on_device(): lax.all_gather(whole_state[None], 'context', axis=0, tiled=True)]
    reduce_scatter x1 -> x0, waiting for transfers between devices: 57.8 us -> none  [on_device(): lax.psum_scatter(jnp.dot(normed_half, w_out, preferred_element_type=jnp.f...]
    dot_general x14 -> x0, matrix products: 34.9 us -> none  [the longest x1 9.01 us: on_device(): jnp.dot(normed_half, w_out, preferred_element_type=jnp.float32)]
    another operation x2 -> x0, loops' own time: 21.7 us -> none  [the longest x1 10.9 us: on_device(): lax.scan(fold_upward, zero_state, (keeps_all, states_all, rank_list))]
    select_n x19 -> x0, other arithmetic: 19.7 us -> none  [the longest x16 18.9 us: fold_upward(): jnp.where(rank_one < my_rank, keep_one[:, None, None] * acc + state_one,...]
    dynamic_slice x32 -> x0, local copies, waits for them, and re-layouts: 18.8 us -> none  [on_device(): lax.scan(fold_upward, zero_state, (keeps_all, states_all, rank_list))]
  transfers between devices with their start and end apart: 10 -> 0, of which waited for: 6 -> 0; matrix products, arithmetic and copies ran while one was open for 20% -> 0% of each run, Pallas kernels for 0% -> 0%
where the time goes in v1:
time: 81.1 us; the launch traced here: 80.8 us
  Pallas kernels  71.5 us (88%)
  local copies, waits for them, and re-layouts  8.72 us (11%)
    pallas_call x1, Pallas kernels, on_device(): pl.pallas_call(layer, out_shape=[jax.ShapeDtypeStruct((OWN_ROWS, MODEL),...  71.5 us
    unnamed x6, local copies, waits for them, and re-layouts  7.72 us

profile of v1, /device:TPU:1, one launch (start us, length us, event | category | flops | bytes accessed | tf_op | source)
XLA Modules:
  0.0 80.8 jit_solution(14601188250633611352)
XLA Ops:
  0.6 71.5 %layer.1 = (bf16[16,8192]{1,0:T(8,128)(2,1)}, bf16[256,512]{1,0:T(8,128)(2,1)}, bf16[256,512]{1,0:T(8,128)(2,1)}, bf16[256,128]{1,0:T(8,128)(2,1)}, f32[8,256]{1,0:T(8,128)}) custom-call(bf16[256,512]{1,0:T(8,128)(2,1)} %x_ref.1, bf16[256,512]{1,0:T(8,128)(2,1)} %gate_ref.1, bf16[256,1024]{1,0:T(8,128)(2,1)} %b_hbm.1, bf16[256,1024]{1,0:T(8,128)(2,1)} %c_hbm.1, ...), custom_call_target="tpu_custom_call" | custom-call | flops 6000000000 | bytes 16000000 | tf_op jit(solution)/shard_map/layer/pallas_call | solution.py:604
  72.1 1.0 %fusion = (bf16[256,64]{1,0:T(8,128)(2,1)S(1)}, bf16[256,64]{1,0:T(8,128)(2,1)S(1)}) fusion(bf16[256,128]{1,0:T(8,128)(2,1)} %get-tuple-element.14), kind=kLoop, calls=%fused_computation | loop fusion | bytes 131072 | tf_op jit(solution)/shard_map/slice | solution.py:718
  73.1 0.7 copy.19
  73.8 0.7 copy.18
  74.5 1.7 %copy.24 = bf16[16,8192]{1,0:T(8,128)(2,1)} copy(bf16[16,8192]{1,0:T(8,128)(2,1)} %get-tuple-element.30) | data formatting | bytes 524288
  76.2 1.7 %copy.25 = bf16[256,512]{1,0:T(8,128)(2,1)} copy(bf16[256,512]{1,0:T(8,128)(2,1)} %get-tuple-element.31) | data formatting | bytes 524288
  77.9 1.7 %copy.26 = bf16[256,512]{1,0:T(8,128)(2,1)} copy(bf16[256,512]{1,0:T(8,128)(2,1)} %get-tuple-element.32) | data formatting | bytes 524288
  79.5 1.3 %copy.27 = f32[8,256]{1,0:T(8,128)} copy(f32[8,256]{1,0:T(8,128)} %get-tuple-element.35) | data formatting | bytes 16384

commit v2 on v1

--- a/solution.py
+++ b/solution.py
@@ -40,29 +40,33 @@
     return lax.dot_general(a, b, (((0,), (0,)), ((), ())), preferred_element_type=F32)
 
 
-def streams(way, hop):
-    if way == 0:
-        return (0, 1) if hop else (0,)
-    return (1, 0) if hop else (1,)
-
-
 def layer(
-    x_ref,
-    gate_ref,
+    x_hbm,
+    gate_hbm,
     b_hbm,
     c_hbm,
-    dt_ref,
+    dt_hbm,
     bias_ref,
     alog_ref,
     skip_ref,
-    gain_ref,
+    gain_hbm,
     w_hbm,
     docs_ref,
     go_hbm,
-    mixed_ref,
+    mixed_out,
+    gx_out,
+    gg_out,
+    gb_out,
+    gc_out,
+    gdt_out,
+    x_ref,
+    gate_ref,
+    dt_ref,
+    gain_ref,
     gx_ref,
     gg_ref,
-    gbc_ref,
+    gb_ref,
+    gc_ref,
     gdt_ref,
     bv,
     cv,
@@ -85,8 +89,8 @@
     sl,
     dsl,
     gcol,
-    wxt,
-    wxn,
+    wxh,
+    cvt,
     fsum,
     keep,
     sb,
@@ -120,6 +124,7 @@
     ob,
     orecv,
     loc,
+    out_s,
     pair_s,
     pair_r,
     ag_s,
@@ -153,12 +158,12 @@
             device_id_type=pl.DeviceIdType.MESH,
         )
 
-    def each(first, last, body):
+    def each(first, last, body, unroll=1):
         def step(i, carry):
             body(i)
             return carry
 
-        lax.fori_loop(first, last, step, 0)
+        lax.fori_loop(first, last, step, 0, unroll=unroll)
 
     barrier = pltpu.get_barrier_semaphore()
 
@@ -175,16 +180,17 @@
 
     here = pl.ds(pl.multiple_of(core * HALF, HALF), HALF)
     there = pl.ds(pl.multiple_of(other * HALF, HALF), HALF)
-    mine = pl.ds(pl.multiple_of(core * OWN_ROWS, OWN_ROWS), OWN_ROWS)
     columns = pl.ds(pl.multiple_of(group * STATE, STATE), STATE)
-    load_go = pltpu.make_async_copy(go_hbm.at[:, here], gbuf.at[chip, mine, :], loc.at[0])
-    load_b = pltpu.make_async_copy(b_hbm.at[:, columns], bv, loc.at[1])
-    load_c = pltpu.make_async_copy(c_hbm.at[:, columns], cv, loc.at[2])
-    load_w = pltpu.make_async_copy(w_hbm.at[:, here], wv.at[core], loc.at[3])
-    load_go.start()
-    load_b.start()
-    load_c.start()
-    load_w.start()
+    load_dt = pltpu.make_async_copy(dt_hbm, dt_ref, loc.at[0])
+    load_x = pltpu.make_async_copy(x_hbm, x_ref, loc.at[1])
+    load_b = pltpu.make_async_copy(b_hbm.at[:, columns], bv, loc.at[2])
+    load_c = pltpu.make_async_copy(c_hbm.at[:, columns], cv, loc.at[3])
+    load_gate = pltpu.make_async_copy(gate_hbm, gate_ref, loc.at[4])
+    load_gain = pltpu.make_async_copy(gain_hbm, gain_ref, loc.at[5])
+    load_go = pltpu.make_async_copy(go_hbm.at[:, here], gbuf.at[chip, core], loc.at[6])
+    load_w = pltpu.make_async_copy(w_hbm.at[:, here], wv.at[core], loc.at[7])
+    for copy in (load_dt, load_x, load_b, load_c, load_gate, load_gain, load_go, load_w):
+        copy.start()
 
     head_rows = lax.broadcasted_iota(jnp.int32, (HEADS, ROWS), 0)
 
@@ -194,6 +200,7 @@
             total = jnp.where(head_rows == h, ref[h], total)
         return total
 
+    load_dt.wait()
     raw = dt_ref[...] + per_head(bias_ref)
     a_rate = -jnp.exp(per_head(alog_ref))
     step = jnp.maximum(raw, 0.0) + jnp.log1p(jnp.exp(-jnp.abs(raw)))
@@ -222,20 +229,25 @@
     step_s[...] = step
     e_s[...] = jnp.where(opening, jnp.exp(running), 0.0)
     wend_s[...] = jnp.where(closing, jnp.exp(final - running), 0.0) * step
-    mask[...] = jnp.where((seg_col == seg_row) & (row_ids <= col_ids), 0.0, -1e30)
-    shifted = (running - jnp.log(step)).T
+    fsum[rank] = jnp.broadcast_to(final, (HEADS, 128))
+
+    load_x.wait()
+    load_b.wait()
+    xt[...] = x_ref[...].T.reshape(HEADS, WIDTH, ROWS)
     for h in range(HEADS):
-        qcol[h] = jnp.broadcast_to(shifted[:, h : h + 1], (ROWS, 128))
-    fsum[rank] = jnp.broadcast_to(final, (HEADS, 128))
-    xt[...] = x_ref[...].T.reshape(HEADS, WIDTH, ROWS)
+        wx = wend_s[h : h + 1, :] * xt[h].astype(F32)
+        wx_hi = wx.astype(BF16)
+        wx_lo = (wx - wx_hi.astype(F32)).astype(BF16)
+        wxh[h] = wx_hi
+        end_state = nn(wx_hi, bv[...]) + nn(wx_lo, bv[...])
+        sb[2 * h : 2 * h + 2] = end_state.astype(BF16).reshape(2, CHUNK, STATE)
+    rb[rank] = sb[rank]
 
     pl.semaphore_wait(barrier, 4 + RANKS - 1)
     pair_go = remote(
-        go_hbm.at[:, there], gbuf.at[chip, mine, :], pair_s.at[0], pair_r.at[0], rank, sibling
+        go_hbm.at[:, there], gbuf.at[chip, core], pair_s.at[0], pair_r.at[0], rank, sibling
     )
     pair_w = remote(w_hbm.at[:, there], wv.at[core], pair_s.at[1], pair_r.at[1], rank, sibling)
-    pair_go.start()
-    pair_w.start()
 
     def spread(which, src, dst, own_src):
         def copy(k):
@@ -256,48 +268,42 @@
     ex_enter = spread(2, eb, s0, False)
     ex_grad = spread(3, sb2, rb2, False)
     ex_later = spread(4, eb2, zz, False)
-    each(1, RANKS, lambda k: ex_keep(k).start())
 
     def ag_copy(hop, way, piece):
         block = (chip + RING - hop) % RING if way == 0 else (chip + hop) % RING
-        cols = pl.ds(piece * PIECE, PIECE)
+        half = core if piece == 0 else other
         slot = (hop * 2 + way) * 2 + piece
+        first = hop == 0 and piece == 0
         return remote(
-            gbuf.at[block, :, cols],
-            gbuf.at[block, :, cols],
+            go_hbm.at[:, here] if first else gbuf.at[block, half],
+            gbuf.at[block, half],
             ag_s.at[slot],
             ag_r.at[slot],
             rank,
             ahead if way == 0 else behind,
         )
 
-    def ag_streams(way, hop):
-        return streams(way, 3 - hop)
-
-    def ag_hop(hop):
+    def ag_step(hop, piece):
         for way in range(2):
-            for piece in ag_streams(way, hop):
+            if hop < 3 or way == piece:
                 if hop:
                     ag_copy(hop - 1, way, piece).wait_recv()
                 ag_copy(hop, way, piece).start()
 
-    load_go.wait()
+    pair_go.start()
+    ag_step(0, 0)
+    each(1, RANKS, lambda k: ex_state(k).start())
+    each(1, RANKS, lambda k: ex_keep(k).start())
+    pair_w.start()
     pair_go.wait_recv()
-    ag_hop(0)
-
-    load_b.wait()
+    ag_step(0, 1)
+
+    mask[...] = jnp.where((seg_col == seg_row) & (row_ids <= col_ids), 0.0, -1e30)
+    shifted = (running - jnp.log(step)).T
+    for h in range(HEADS):
+        qcol[h] = jnp.broadcast_to(shifted[:, h : h + 1], (ROWS, 128))
+
     load_c.wait()
-    for h in range(HEADS):
-        wxt[h] = wend_s[h : h + 1, :] * xt[h].astype(F32)
-    wx_all = wxt[...].reshape(CHANNELS, ROWS)
-    wx_hi = wx_all.astype(BF16)
-    wx_lo = (wx_all - wx_hi.astype(F32)).astype(BF16)
-    end_state = nn(wx_hi, bv[...]) + nn(wx_lo, bv[...])
-    sb[...] = end_state.astype(BF16).reshape(RANKS, CHUNK, STATE)
-    each(1, RANKS, lambda k: ex_state(k).start())
-    rb[rank] = sb[rank]
-    wxn[...] = wx_hi.T
-
     gt[...] = nt(bv[...], cv[...])
 
     def inside(h):
@@ -308,8 +314,8 @@
         mt[h] = mixing
         yin[h] = nn(xt[h], mixing)
 
-    each(0, HEADS, inside)
-    ag_hop(1)
+    each(0, HEADS, inside, 2)
+    ag_step(1, 0)
 
     each(1, RANKS, lambda k: ex_keep(k).wait_recv())
     for r in range(RANKS):
@@ -332,7 +338,10 @@
         total = keep_of(r) * total + rb[r].astype(F32)
     each(1, RANKS, lambda k: ex_enter(k).start())
     s0[rank] = eb[rank]
-
+    ag_step(1, 1)
+
+    load_gate.wait()
+    load_gain.wait()
     v = gate_ref[...].T.astype(F32)
     sig = 1.0 / (1.0 + jnp.exp(-v))
     sl[...] = (v * sig).reshape(HEADS, WIDTH, ROWS)
@@ -343,7 +352,9 @@
         picked = jnp.where(eye[:128, :128], line, 0.0)
         column = jnp.sum(picked, axis=1, keepdims=True)
         gcol[2 * q : 2 * q + 2] = jnp.broadcast_to(column, (128, 128)).reshape(2, WIDTH, 128)
-    ag_hop(2)
+    cvt[...] = cv[...].T
+    ag_step(2, 0)
+    ag_step(2, 1)
 
     each(1, RANKS, lambda k: ex_enter(k).wait_recv())
     enter_all = s0[...].reshape(CHANNELS, STATE)
@@ -374,11 +385,14 @@
     for x in (1, 2, 3):
         mate_copy(0, nbuf, x).start()
     gain_full = jnp.concatenate([gcol[...], gcol[...]], axis=2)
-    scaled = (gated[...] * gain_full).reshape(CHANNELS, ROWS).astype(BF16)
-    gn[core] = scaled.T
+    scaled = (gated[...] * gain_full).reshape(CHANNELS, ROWS)
+    scaled_hi = scaled.astype(BF16)
+    scaled_lo = (scaled - scaled_hi.astype(F32)).astype(BF16)
+    gn[core, 0] = scaled_hi.T
+    gn[core, 1] = scaled_lo.T
     pair_gn = remote(gn.at[core], gn.at[core], pair_s.at[2], pair_r.at[2], rank, sibling)
     pair_gn.start()
-    ag_hop(3)
+    ag_step(3, 0)
 
     load_w.wait()
     pair_w.wait_recv()
@@ -387,10 +401,36 @@
 
     def product(n):
         cols = pl.ds(pl.multiple_of(n * tile, tile), tile)
-        value = nn(gn[0], wv[0, :, cols]) + nn(gn[1], wv[1, :, cols])
+        value = jnp.zeros((ROWS, tile), F32)
+        for one in range(2):
+            for part in range(2):
+                value = value + nn(gn[one, part], wv[one, :, cols])
         pp[:, :, cols] = value.reshape(RING, CHIP_ROWS, tile)
 
-    each(0, HALF // tile, product)
+    each(0, HALF // tile // 2, product)
+    ag_step(3, 1)
+    each(HALF // tile // 2, HALF // tile, product)
+
+    load_go.wait()
+    for way in range(2):
+        for piece in range(2):
+            ag_copy(3 if way == piece else 2, way, piece).wait_recv()
+
+    def fold(n, total):
+        cols = pl.ds(pl.multiple_of(n * tile, tile), tile)
+        both = gbuf[:, :, :, cols].reshape(ROWS, tile).astype(F32) * pp[:, :, cols].reshape(
+            ROWS, tile
+        )
+        for i in range(tile // 128):
+            total = total + both[:, i * 128 : (i + 1) * 128]
+        return total
+
+    along_col = jnp.sum(
+        lax.fori_loop(0, HALF // tile, fold, jnp.zeros((ROWS, 128), F32)), axis=1, keepdims=True
+    )
+    abuf[0] = jnp.sum(jnp.where(eye, along_col, 0.0), axis=0, keepdims=True)
+    for x in (1, 2, 3):
+        mate_copy(1, abuf, x).start()
     for x in (1, 2, 3):
         mate_copy(0, nbuf, x).wait_recv()
     mean = (nbuf[0] + nbuf[1] + nbuf[2] + nbuf[3]) * (1.0 / GROUP_CHANNELS)
@@ -416,38 +456,28 @@
             ahead if way == 0 else behind,
         )
 
-    def rs_hop(hop):
+    def rs_step(hop, turn):
         for way in range(2):
+            piece = (way + turn) % 2
             block = (chip + 4 - hop) % RING if way == 0 else (chip + 4 + hop) % RING
-            for piece in streams(way, hop):
-                cols = pl.ds(piece * PIECE, PIECE)
-                value = own_part(block, piece)
-                if hop and piece in streams(way, hop - 1):
-                    rs_copy(hop - 1, way, piece).wait_recv()
-                    value = value + rrecv[way, hop - 1, :, cols].astype(F32)
-                rsend[way, hop, :, cols] = value.astype(BF16)
-                rs_copy(hop, way, piece).start()
-
-    rs_hop(0)
-
-    for way in range(2):
-        for piece in range(2):
-            hop = 3 if piece in ag_streams(way, 3) else 2
-            ag_copy(hop, way, piece).wait_recv()
+            cols = pl.ds(piece * PIECE, PIECE)
+            value = own_part(block, piece)
+            if hop > turn:
+                rs_copy(hop - 1, way, piece).wait_recv()
+                value = value + rrecv[way, hop - 1, :, cols].astype(F32)
+            rsend[way, hop, :, cols] = value.astype(BF16)
+            rs_copy(hop, way, piece).start()
+
+    rs_step(0, 0)
+
     cotangent = gbuf[...].reshape(ROWS, HALF)
     qsend[...] = nt(wv[other], cotangent)
     pair_q = remote(qsend, qrecv, pair_s.at[3], pair_r.at[3], rank, sibling)
     pair_q.start()
+    rs_step(1, 1)
     grad_own = nt(wv[core], cotangent)
-    rs_hop(1)
     pair_q.wait_recv()
     grad_scaled = (grad_own + qrecv[...]).reshape(HEADS, WIDTH, ROWS) * gain_full
-    along = jnp.sum(
-        (grad_scaled * gated[...]).reshape(CHANNELS, ROWS), axis=0, keepdims=True
-    )
-    abuf[0] = along
-    for x in (1, 2, 3):
-        mate_copy(1, abuf, x).start()
     for x in (1, 2, 3):
         mate_copy(1, abuf, x).wait_recv()
     along = abuf[0] + abuf[1] + abuf[2] + abuf[3]
@@ -456,14 +486,20 @@
     dy_all = grad_gated * sl[...]
     dyb[...] = dy_all.astype(BF16)
     grad_gate = (grad_gated * yt[...] * dsl[...]).astype(BF16)
-    gg_ref[...] = grad_gate.reshape(CHANNELS, ROWS).T
-
     for h in range(HEADS):
         edy[h] = (e_s[h : h + 1, :] * dyb[h].astype(F32)).astype(BF16)
     edy_all = edy[...].reshape(CHANNELS, ROWS)
     sb2[...] = nn(edy_all, cv[...]).astype(BF16).reshape(RANKS, CHUNK, STATE)
     each(1, RANKS, lambda k: ex_grad(k).start())
     rb2[rank] = sb2[rank]
+    rs_step(1, 0)
+    gg_ref[...] = grad_gate.reshape(CHANNELS, ROWS).T
+
+    def leave(which, source, target):
+        return pltpu.make_async_copy(source, target, out_s.at[which])
+
+    leave_gg = leave(0, gg_ref, gg_out)
+    leave_gg.start()
 
     dgt[...] = jnp.zeros((ROWS, ROWS), F32)
 
@@ -478,8 +514,9 @@
         cardot[pl.ds(h, 1), :] = jnp.sum(dyf * car[h], axis=0, keepdims=True)
         coldot[pl.ds(h, 1), :] = jnp.sum(x_now.astype(F32) * grad_in, axis=0, keepdims=True)
 
-    each(0, HEADS, back)
-    rs_hop(2)
+    each(0, HEADS, back, 2)
+    rs_step(2, 1)
+    rs_step(2, 0)
 
     each(1, RANKS, lambda k: ex_grad(k).wait_recv())
     total = jnp.zeros((CHUNK, STATE), F32)
@@ -489,34 +526,38 @@
     each(1, RANKS, lambda k: ex_later(k).start())
     zz[rank] = eb2[rank]
 
-    grad_scores = dgt[...].astype(BF16)
-    grad_c = tn(grad_scores, bv[...]) + nn(edy_all.T, enter_all)
-    grad_b = nn(grad_scores, cv[...])
-    rs_hop(3)
-
-    each(1, RANKS, lambda k: ex_later(k).wait_recv())
-    later = zz[...].reshape(CHANNELS, STATE)
-    grad_b = grad_b + nn(wxn[...], later)
-    lane = lax.broadcasted_iota(jnp.int32, (ROWS, 128), 1)
-    for q in range(2):
-        tile_b = grad_b[:, q * 128 : (q + 1) * 128]
-        tile_c = grad_c[:, q * 128 : (q + 1) * 128]
-        gown[2 * q] = jnp.where(lane < 64, tile_b, pltpu.roll(tile_c, 64, 1))
-        gown[2 * q + 1] = jnp.where(lane < 64, pltpu.roll(tile_b, 64, 1), tile_c)
-    gsend[...] = gown[...].astype(BF16)
-
-    def share_copy(x):
+    def share_copy(which, x):
         return remote(
-            gsend.at[mates[x]],
-            grecv.at[x],
-            gr_s.at[2, x],
-            gr_r.at[2, x],
+            gsend.at[which, mates[x]],
+            grecv.at[which, x],
+            gr_s.at[2 + which, x],
+            gr_r.at[2 + which, x],
             rank,
             group * 4 + mates[x],
         )
 
+    grad_scores = dgt[...].astype(BF16)
+    grad_c = tn(bv[...], grad_scores) + tn(enter_all, edy_all)
+    gown[1] = grad_c.reshape(4, WIDTH, ROWS)
+    gsend[1] = gown[1].astype(BF16)
     for x in (1, 2, 3):
-        share_copy(x).start()
+        share_copy(1, x).start()
+    grad_b = nt(cvt[...], grad_scores)
+    from_here = jnp.where(row_ids >= col_ids, 1.0, 0.0)
+    before = jnp.where(row_ids < col_ids, 1.0, 0.0)
+    kept = jnp.where(seg_last == 0, 1.0, 0.0) * jnp.exp(final)
+    grad_rate = nn(rowdot[...] - coldot[...] + cardot[...], from_here, HIGH)
+
+    rs_step(3, 1)
+    rs_step(3, 0)
+
+    each(1, RANKS, lambda k: ex_later(k).wait_recv())
+    later = zz[...].reshape(CHANNELS, STATE)
+    grad_b = grad_b + tn(later, wxh[...].reshape(CHANNELS, ROWS))
+    gown[0] = grad_b.reshape(4, WIDTH, ROWS)
+    gsend[0] = gown[0].astype(BF16)
+    for x in (1, 2, 3):
+        share_copy(0, x).start()
 
     moved_back = nt(later, bv[...])
     inner = jnp.zeros((HEADS, ROWS), F32)
@@ -530,21 +571,16 @@
         block = overlap[h * WIDTH : (h + 1) * WIDTH, :]
         inner = jnp.where(head_rows == h, jnp.sum(block), inner)
     gx_ref[...] = dxin[...].reshape(CHANNELS, ROWS).astype(BF16).T
-
-    from_here = jnp.where(row_ids >= col_ids, 1.0, 0.0)
-    before = jnp.where(row_ids < col_ids, 1.0, 0.0)
-    kept = jnp.where(seg_last == 0, 1.0, 0.0) * jnp.exp(final)
-    grad_rate = (
-        nn(rowdot[...] - coldot[...] + cardot[...], from_here, HIGH)
-        + nn(zdot[...], before, HIGH)
-        + kept * inner
-    )
+    leave_gx = leave(2, gx_ref, gx_out)
+    leave_gx.start()
+    grad_rate = grad_rate + nn(zdot[...], before, HIGH) + kept * inner
     grad_step = (coldot[...] + zdot[...]) / step_s[...] + a_rate * grad_rate
     gdt_ref[...] = grad_step * (1.0 / (1.0 + jnp.exp(-raw)))
-
-    for way in range(2):
-        for piece in range(2):
-            rs_copy(3, way, piece).wait_recv()
+    leave_dt = leave(3, gdt_ref, gdt_out)
+    leave_dt.start()
+    for turn in (1, 0):
+        for way in range(2):
+            rs_copy(3, way, (way + turn) % 2).wait_recv()
     for piece in range(2):
         cols = pl.ds(piece * PIECE, PIECE)
         value = (
@@ -555,30 +591,51 @@
         ob[:, :, cols] = value.astype(BF16).reshape(2, OWN_ROWS, PIECE)
     pair_out = remote(ob.at[other], orecv, pair_s.at[4], pair_r.at[4], rank, sibling)
     pair_out.start()
-    mixed_ref[:, here] = ob[core]
-    for x in (1, 2, 3):
-        share_copy(x).wait_recv()
-    shares = gown[member]
-    for x in (1, 2, 3):
-        shares = shares + grecv[x].astype(F32)
-    gbc_ref[...] = shares.astype(BF16)
+    leave_mine = leave(1, ob.at[core], mixed_out.at[:, here])
+    leave_mine.start()
+
     pair_out.wait_recv()
-    mixed_ref[:, there] = orecv[...]
+    leave_theirs = leave(4, orecv, mixed_out.at[:, there])
+    leave_theirs.start()
+
+    def gather(which):
+        for x in (1, 2, 3):
+            share_copy(which, x).wait_recv()
+        shares = gown[which, member]
+        for x in (1, 2, 3):
+            shares = shares + grecv[which, x].astype(F32)
+        return shares.astype(BF16)
+
+    gc_ref[...] = gather(1)
+    leave_gc = leave(5, gc_ref, gc_out)
+    leave_gc.start()
+    gb_ref[...] = gather(0)
+    leave_gb = leave(6, gb_ref, gb_out)
+    leave_gb.start()
 
     for copy in (pair_go, pair_w, pair_gn, pair_q, pair_out):
         copy.wait_send()
     for hop in range(4):
         for way in range(2):
-            for piece in ag_streams(way, hop):
-                ag_copy(hop, way, piece).wait_send()
-            for piece in streams(way, hop):
-                rs_copy(hop, way, piece).wait_send()
+            for piece in range(2):
+                if hop < 3 or way == piece:
+                    ag_copy(hop, way, piece).wait_send()
+                if hop or way == piece:
+                    rs_copy(hop, way, piece).wait_send()
     for exchange in (ex_keep, ex_state, ex_enter, ex_grad, ex_later):
         each(1, RANKS, lambda k: exchange(k).wait_send())
     for x in (1, 2, 3):
         mate_copy(0, nbuf, x).wait_send()
         mate_copy(1, abuf, x).wait_send()
-        share_copy(x).wait_send()
+        share_copy(0, x).wait_send()
+        share_copy(1, x).wait_send()
+    for copy in (leave_gg, leave_mine, leave_gx, leave_dt, leave_theirs, leave_gc, leave_gb):
+        copy.wait()
+
+
+def hand_out(*refs):
+    for source, target in zip(refs[:6], refs[6:]):
+        target[...] = source[...]
 
 
 def on_device(
@@ -607,29 +664,39 @@
             jax.ShapeDtypeStruct((OWN_ROWS, MODEL), BF16),
             jax.ShapeDtypeStruct((ROWS, CHANNELS), BF16),
             jax.ShapeDtypeStruct((ROWS, CHANNELS), BF16),
-            jax.ShapeDtypeStruct((ROWS, 128), BF16),
+            jax.ShapeDtypeStruct((WIDTH, ROWS), BF16),
+            jax.ShapeDtypeStruct((WIDTH, ROWS), BF16),
             jax.ShapeDtypeStruct((HEADS, ROWS), F32),
         ],
         in_specs=[
-            vmem,
-            vmem,
             anywhere,
             anywhere,
-            vmem,
+            anywhere,
+            anywhere,
+            anywhere,
             smem,
             smem,
             smem,
-            vmem,
+            anywhere,
             anywhere,
             smem,
             anywhere,
         ],
-        out_specs=[vmem] * 5,
+        out_specs=[anywhere] * 6,
         scratch_shapes=[
+            pltpu.VMEM((ROWS, CHANNELS), BF16),
+            pltpu.VMEM((ROWS, CHANNELS), BF16),
+            pltpu.VMEM((HEADS, ROWS), F32),
+            pltpu.VMEM((1, CHANNELS), F32),
+            pltpu.VMEM((ROWS, CHANNELS), BF16),
+            pltpu.VMEM((ROWS, CHANNELS), BF16),
+            pltpu.VMEM((WIDTH, ROWS), BF16),
+            pltpu.VMEM((WIDTH, ROWS), BF16),
+            pltpu.VMEM((HEADS, ROWS), F32),
             pltpu.VMEM((ROWS, STATE), BF16),
             pltpu.VMEM((ROWS, STATE), BF16),
             pltpu.VMEM((2, CHANNELS, HALF), BF16),
-            pltpu.VMEM((RING, CHIP_ROWS, HALF), BF16),
+            pltpu.VMEM((RING, 2, OWN_ROWS, HALF), BF16),
             pltpu.VMEM(by_head, BF16),
             pltpu.VMEM((HEADS, ROWS), F32),
             pltpu.VMEM((HEADS, ROWS), F32),
@@ -647,8 +714,8 @@
             pltpu.VMEM(by_head, F32),
             pltpu.VMEM(by_head, F32),
             pltpu.VMEM((HEADS, WIDTH, 128), F32),
-            pltpu.VMEM(by_head, F32),
-            pltpu.VMEM((ROWS, CHANNELS), BF16),
+            pltpu.VMEM(by_head, BF16),
+            pltpu.VMEM((STATE, ROWS), BF16),
             pltpu.VMEM((RANKS, HEADS, 128), F32),
             pltpu.VMEM((RANKS, HEADS, 128), F32),
             pltpu.VMEM(by_rank, BF16),
@@ -659,7 +726,7 @@
             pltpu.VMEM(by_rank, BF16),
             pltpu.VMEM(by_rank, BF16),
             pltpu.VMEM(by_rank, BF16),
-            pltpu.VMEM((2, ROWS, CHANNELS), BF16),
+            pltpu.VMEM((2, 2, ROWS, CHANNELS), BF16),
             pltpu.VMEM((4, 1, ROWS), F32),
             pltpu.VMEM((4, 1, ROWS), F32),
             pltpu.VMEM((RING, CHIP_ROWS, 128), F32),
@@ -676,12 +743,13 @@
             pltpu.VMEM((HEADS, ROWS), F32),
             pltpu.VMEM((HEADS, ROWS), F32),
             pltpu.VMEM((HEADS, ROWS), F32),
-            pltpu.VMEM((4, ROWS, 128), F32),
-            pltpu.VMEM((4, ROWS, 128), BF16),
-            pltpu.VMEM((4, ROWS, 128), BF16),
+            pltpu.VMEM((2, 4, WIDTH, ROWS), F32),
+            pltpu.VMEM((2, 4, WIDTH, ROWS), BF16),
+            pltpu.VMEM((2, 4, WIDTH, ROWS), BF16),
             pltpu.VMEM((2, OWN_ROWS, HALF), BF16),
             pltpu.VMEM((OWN_ROWS, HALF), BF16),
-            dma((4,)),
+            dma((8,)),
+            dma((7,)),
             dma((5,)),
             dma((5,)),
             dma((16,)),
@@ -690,8 +758,8 @@
             dma((16,)),
             dma((5, RANKS)),
             dma((5, RANKS)),
-            dma((3, 4)),
-            dma((3, 4)),
+            dma((4, 4)),
+            dma((4, 4)),
         ],
         compiler_params=pltpu.CompilerParams(
             collective_id=0, has_side_effects=True, vmem_limit_bytes=56 * 1024 * 1024
@@ -714,8 +782,14 @@
         doc_starts,
         grad_out,
     )
-    mixed, grad_x, grad_gate, grad_bc, grad_dt = out
-    return (mixed, grad_x, grad_gate, grad_bc[:, :64], grad_bc[:, 64:], grad_dt)
+    mixed, grad_x, grad_gate, grad_b, grad_c, grad_dt = pl.pallas_call(
+        hand_out,
+        out_shape=[jax.ShapeDtypeStruct(o.shape, o.dtype) for o in out],
+        in_specs=[vmem] * 6,
+        out_specs=[vmem] * 6,
+        name="hand_out",
+    )(*out)
+    return (mixed, grad_x, grad_gate, grad_b.T, grad_c.T, grad_dt)
 
 
 def solution(mesh):

time: 81.1 us -> 69.7 us (0.86)
  local copies, waits for them, and re-layouts: 8.72 us -> 0 us
  Pallas kernels: 71.5 us -> 68.9 us
    unnamed x6 -> x0, local copies, waits for them, and re-layouts: 7.72 us -> none
    pallas_call x1, Pallas kernels: 71.5 us -> 66.8 us  [on_device(): pl.pallas_call(layer, out_shape=[jax.ShapeDtypeStruct((OWN_ROWS, MODEL),...]
    pallas_call x0 -> x1, Pallas kernels: none -> 2.04 us  [on_device(): pl.pallas_call(hand_out, out_shape=[jax.ShapeDtypeStruct(o.shape, o.dtype...]
    slice x1 -> x0, local copies, waits for them, and re-layouts: 1 us -> none  [on_device(): return (mixed, grad_x, grad_gate, grad_bc[:, :64], grad_bc[:, 64:], grad_dt)]
where the time goes in v2:
time: 69.7 us; the launch traced here: 69.5 us
  Pallas kernels  68.9 us (99%)
    pallas_call x1, Pallas kernels, on_device(): pl.pallas_call(layer, out_shape=[jax.ShapeDtypeStruct((OWN_ROWS, MODEL),...  66.8 us
    pallas_call x1, Pallas kernels, on_device(): pl.pallas_call(hand_out, out_shape=[jax.ShapeDtypeStruct(o.shape, o.dtype...  2.04 us

profile of v2, /device:TPU:1, one launch (start us, length us, event | category | flops | bytes accessed | tf_op | source)
XLA Modules:
  0.0 69.5 jit_solution(12632634439820320436)
XLA Ops:
  0.6 66.8 %layer.1 = (bf16[16,8192]{1,0:T(8,128)(2,1)}, bf16[256,512]{1,0:T(8,128)(2,1)}, bf16[256,512]{1,0:T(8,128)(2,1)}, bf16[64,256]{1,0:T(8,128)(2,1)}, bf16[64,256]{1,0:T(8,128)(2,1)}, /*index=5*/f32[8,256]{1,0:T(8,128)}) custom-call(bf16[256,512]{1,0:T(8,128)(2,1)} %x_hbm.1, bf16[256,512]{1,0:T(8,128)(2,1)} %gate_hbm.1, bf16[256,1024]{1,0:T(8,128)(2,1)} %b_hbm.1, ...), custom_call_target="tpu_custom_call" | custom-call | flops 6000000000 | bytes 16000000 | tf_op jit(solution)/shard_map/layer/pallas_call | solution.py:661
  67.5 2.0 %hand_out.1 = (bf16[16,8192]{1,0:T(8,128)(2,1)}, bf16[256,512]{1,0:T(8,128)(2,1)}, bf16[256,512]{1,0:T(8,128)(2,1)}, bf16[64,256]{1,0:T(8,128)(2,1)}, bf16[64,256]{1,0:T(8,128)(2,1)}, /*index=5*/f32[8,256]{1,0:T(8,128)}) custom-call(bf16[16,8192]{1,0:T(8,128)(2,1)} %get-tuple-element.18.refs_0_, bf16[256,512]{1,0:T(8,128)(2,1)} %get-tuple-element.19.refs_1_, ...), custom_call_target="tpu_custom_call" | custom-call | tf_op jit(solution)/shard_map/hand_out/pallas_call | solution.py:785

commit v3 on v2

--- a/solution.py
+++ b/solution.py
@@ -22,6 +22,7 @@
 OWN_ROWS = CHIP_ROWS // 2
 PIECE = HALF // 2
 CHUNK = CHANNELS // RANKS
+TAIL = 16
 GROUP_CHANNELS = 2048
 EPS = 1e-05
 
@@ -91,7 +92,6 @@
     gcol,
     wxh,
     cvt,
-    fsum,
     keep,
     sb,
     rb,
@@ -229,7 +229,10 @@
     step_s[...] = step
     e_s[...] = jnp.where(opening, jnp.exp(running), 0.0)
     wend_s[...] = jnp.where(closing, jnp.exp(final - running), 0.0) * step
-    fsum[rank] = jnp.broadcast_to(final, (HEADS, 128))
+    final_hi = final.astype(BF16).astype(F32)
+    final_mid = (final - final_hi).astype(BF16).astype(F32)
+    final_lo = final - final_hi - final_mid
+    tail_rows = lax.broadcasted_iota(jnp.int32, (TAIL, STATE), 0)
 
     load_x.wait()
     load_b.wait()
@@ -240,7 +243,18 @@
         wx_lo = (wx - wx_hi.astype(F32)).astype(BF16)
         wxh[h] = wx_hi
         end_state = nn(wx_hi, bv[...]) + nn(wx_lo, bv[...])
-        sb[2 * h : 2 * h + 2] = end_state.astype(BF16).reshape(2, CHUNK, STATE)
+        sb[2 * h : 2 * h + 2, :CHUNK] = end_state.astype(BF16).reshape(2, CHUNK, STATE)
+        terms = jnp.where(
+            tail_rows == 0,
+            final_hi[h : h + 1],
+            jnp.where(
+                tail_rows == 1,
+                final_mid[h : h + 1],
+                jnp.where(tail_rows == 2, final_lo[h : h + 1], 0.0),
+            ),
+        ).astype(BF16)
+        sb[2 * h, CHUNK:] = terms
+        sb[2 * h + 1, CHUNK:] = terms
     rb[rank] = sb[rank]
 
     pl.semaphore_wait(barrier, 4 + RANKS - 1)
@@ -249,11 +263,11 @@
     )
     pair_w = remote(w_hbm.at[:, there], wv.at[core], pair_s.at[1], pair_r.at[1], rank, sibling)
 
-    def spread(which, src, dst, own_src):
+    def spread(which, src, dst):
         def copy(k):
             to = (rank + k) % RANKS
             return remote(
-                src.at[rank] if own_src else src.at[to],
+                src.at[to],
                 dst.at[rank],
                 ex_s.at[which, k],
                 ex_r.at[which, k],
@@ -263,11 +277,10 @@
 
         return copy
 
-    ex_keep = spread(0, fsum, fsum, True)
-    ex_state = spread(1, sb, rb, False)
-    ex_enter = spread(2, eb, s0, False)
-    ex_grad = spread(3, sb2, rb2, False)
-    ex_later = spread(4, eb2, zz, False)
+    ex_state = spread(0, sb, rb)
+    ex_enter = spread(1, eb, s0)
+    ex_grad = spread(2, sb2, rb2)
+    ex_later = spread(3, eb2, zz)
 
     def ag_copy(hop, way, piece):
         block = (chip + RING - hop) % RING if way == 0 else (chip + hop) % RING
@@ -293,11 +306,30 @@
     pair_go.start()
     ag_step(0, 0)
     each(1, RANKS, lambda k: ex_state(k).start())
-    each(1, RANKS, lambda k: ex_keep(k).start())
     pair_w.start()
     pair_go.wait_recv()
     ag_step(0, 1)
 
+    def keep_of(r):
+        return keep[r]
+
+    each(1, RANKS, lambda k: ex_state(k).wait_recv())
+    for r in range(RANKS):
+        count = jnp.int32(0)
+        for i in range(4):
+            begin = docs_ref[i]
+            count = count + jnp.where((begin >= r * ROWS) & (begin < (r + 1) * ROWS), 1, 0)
+        whole = jnp.where(count == 0, 1.0, 0.0)
+        terms = rb[r, CHUNK:].astype(F32)
+        keep[r] = jnp.exp(terms[0:1] + terms[1:2] + terms[2:3]) * whole
+    total = jnp.zeros((CHUNK, STATE), F32)
+    for r in range(RANKS):
+        eb[r] = total.astype(BF16)
+        total = keep_of(r) * total + rb[r, :CHUNK].astype(F32)
+    each(1, RANKS, lambda k: ex_enter(k).start())
+    s0[rank] = eb[rank]
+
+    ag_step(1, 0)
     mask[...] = jnp.where((seg_col == seg_row) & (row_ids <= col_ids), 0.0, -1e30)
     shifted = (running - jnp.log(step)).T
     for h in range(HEADS):
@@ -314,31 +346,9 @@
         mt[h] = mixing
         yin[h] = nn(xt[h], mixing)
 
-    each(0, HEADS, inside, 2)
-    ag_step(1, 0)
-
-    each(1, RANKS, lambda k: ex_keep(k).wait_recv())
-    for r in range(RANKS):
-        count = jnp.int32(0)
-        for i in range(4):
-            begin = docs_ref[i]
-            count = count + jnp.where((begin >= r * ROWS) & (begin < (r + 1) * ROWS), 1, 0)
-        whole = jnp.where(count == 0, 1.0, 0.0)
-        keep[r] = jnp.exp(fsum[r]) * whole
-    my_head = rank // 2
-
-    def keep_of(r):
-        row = keep[r, pl.ds(my_head, 1), :]
-        return jnp.concatenate([row, row], axis=1)
-
-    each(1, RANKS, lambda k: ex_state(k).wait_recv())
-    total = jnp.zeros((CHUNK, STATE), F32)
-    for r in range(RANKS):
-        eb[r] = total.astype(BF16)
-        total = keep_of(r) * total + rb[r].astype(F32)
-    each(1, RANKS, lambda k: ex_enter(k).start())
-    s0[rank] = eb[rank]
+    each(0, HEADS // 2, inside, 2)
     ag_step(1, 1)
+    each(HEADS // 2, HEADS, inside, 2)
 
     load_gate.wait()
     load_gain.wait()
@@ -353,10 +363,9 @@
         column = jnp.sum(picked, axis=1, keepdims=True)
         gcol[2 * q : 2 * q + 2] = jnp.broadcast_to(column, (128, 128)).reshape(2, WIDTH, 128)
     cvt[...] = cv[...].T
+
+    each(1, RANKS, lambda k: ex_enter(k).wait_recv())
     ag_step(2, 0)
-    ag_step(2, 1)
-
-    each(1, RANKS, lambda k: ex_enter(k).wait_recv())
     enter_all = s0[...].reshape(CHANNELS, STATE)
     car[...] = nt(enter_all, cv[...]).reshape(HEADS, WIDTH, ROWS)
 
@@ -386,13 +395,10 @@
         mate_copy(0, nbuf, x).start()
     gain_full = jnp.concatenate([gcol[...], gcol[...]], axis=2)
     scaled = (gated[...] * gain_full).reshape(CHANNELS, ROWS)
-    scaled_hi = scaled.astype(BF16)
-    scaled_lo = (scaled - scaled_hi.astype(F32)).astype(BF16)
-    gn[core, 0] = scaled_hi.T
-    gn[core, 1] = scaled_lo.T
+    gn[core] = scaled.astype(BF16).T
     pair_gn = remote(gn.at[core], gn.at[core], pair_s.at[2], pair_r.at[2], rank, sibling)
     pair_gn.start()
-    ag_step(3, 0)
+    ag_step(2, 1)
 
     load_w.wait()
     pair_w.wait_recv()
@@ -403,34 +409,14 @@
         cols = pl.ds(pl.multiple_of(n * tile, tile), tile)
         value = jnp.zeros((ROWS, tile), F32)
         for one in range(2):
-            for part in range(2):
-                value = value + nn(gn[one, part], wv[one, :, cols])
+            value = value + nn(gn[one], wv[one, :, cols])
         pp[:, :, cols] = value.reshape(RING, CHIP_ROWS, tile)
 
     each(0, HALF // tile // 2, product)
+    ag_step(3, 0)
+    each(HALF // tile // 2, HALF // tile, product)
     ag_step(3, 1)
-    each(HALF // tile // 2, HALF // tile, product)
-
-    load_go.wait()
-    for way in range(2):
-        for piece in range(2):
-            ag_copy(3 if way == piece else 2, way, piece).wait_recv()
-
-    def fold(n, total):
-        cols = pl.ds(pl.multiple_of(n * tile, tile), tile)
-        both = gbuf[:, :, :, cols].reshape(ROWS, tile).astype(F32) * pp[:, :, cols].reshape(
-            ROWS, tile
-        )
-        for i in range(tile // 128):
-            total = total + both[:, i * 128 : (i + 1) * 128]
-        return total
-
-    along_col = jnp.sum(
-        lax.fori_loop(0, HALF // tile, fold, jnp.zeros((ROWS, 128), F32)), axis=1, keepdims=True
-    )
-    abuf[0] = jnp.sum(jnp.where(eye, along_col, 0.0), axis=0, keepdims=True)
-    for x in (1, 2, 3):
-        mate_copy(1, abuf, x).start()
+
     for x in (1, 2, 3):
         mate_copy(0, nbuf, x).wait_recv()
     mean = (nbuf[0] + nbuf[1] + nbuf[2] + nbuf[3]) * (1.0 / GROUP_CHANNELS)
@@ -470,11 +456,33 @@
 
     rs_step(0, 0)
 
+    load_go.wait()
+    for way in range(2):
+        for piece in range(2):
+            ag_copy(3 if way == piece else 2, way, piece).wait_recv()
+
+    def fold(n, total):
+        cols = pl.ds(pl.multiple_of(n * tile, tile), tile)
+        both = gbuf[:, :, :, cols].reshape(ROWS, tile).astype(F32) * pp[:, :, cols].reshape(
+            ROWS, tile
+        )
+        for i in range(tile // 128):
+            total = total + both[:, i * 128 : (i + 1) * 128]
+        return total
+
+    along_col = jnp.sum(
+        lax.fori_loop(0, HALF // tile, fold, jnp.zeros((ROWS, 128), F32)), axis=1, keepdims=True
+    )
+    abuf[0] = jnp.sum(jnp.where(eye, along_col, 0.0), axis=0, keepdims=True)
+    for x in (1, 2, 3):
+        mate_copy(1, abuf, x).start()
+    rs_step(1, 1)
+
     cotangent = gbuf[...].reshape(ROWS, HALF)
     qsend[...] = nt(wv[other], cotangent)
     pair_q = remote(qsend, qrecv, pair_s.at[3], pair_r.at[3], rank, sibling)
     pair_q.start()
-    rs_step(1, 1)
+    rs_step(1, 0)
     grad_own = nt(wv[core], cotangent)
     pair_q.wait_recv()
     grad_scaled = (grad_own + qrecv[...]).reshape(HEADS, WIDTH, ROWS) * gain_full
@@ -492,7 +500,7 @@
     sb2[...] = nn(edy_all, cv[...]).astype(BF16).reshape(RANKS, CHUNK, STATE)
     each(1, RANKS, lambda k: ex_grad(k).start())
     rb2[rank] = sb2[rank]
-    rs_step(1, 0)
+    rs_step(2, 1)
     gg_ref[...] = grad_gate.reshape(CHANNELS, ROWS).T
 
     def leave(which, source, target):
@@ -515,7 +523,6 @@
         coldot[pl.ds(h, 1), :] = jnp.sum(x_now.astype(F32) * grad_in, axis=0, keepdims=True)
 
     each(0, HEADS, back, 2)
-    rs_step(2, 1)
     rs_step(2, 0)
 
     each(1, RANKS, lambda k: ex_grad(k).wait_recv())
@@ -525,6 +532,7 @@
         total = keep_of(r) * total + rb2[r].astype(F32)
     each(1, RANKS, lambda k: ex_later(k).start())
     zz[rank] = eb2[rank]
+    rs_step(3, 1)
 
     def share_copy(which, x):
         return remote(
@@ -548,7 +556,6 @@
     kept = jnp.where(seg_last == 0, 1.0, 0.0) * jnp.exp(final)
     grad_rate = nn(rowdot[...] - coldot[...] + cardot[...], from_here, HIGH)
 
-    rs_step(3, 1)
     rs_step(3, 0)
 
     each(1, RANKS, lambda k: ex_later(k).wait_recv())
@@ -622,7 +629,7 @@
                     ag_copy(hop, way, piece).wait_send()
                 if hop or way == piece:
                     rs_copy(hop, way, piece).wait_send()
-    for exchange in (ex_keep, ex_state, ex_enter, ex_grad, ex_later):
+    for exchange in (ex_state, ex_enter, ex_grad, ex_later):
         each(1, RANKS, lambda k: exchange(k).wait_send())
     for x in (1, 2, 3):
         mate_copy(0, nbuf, x).wait_send()
@@ -716,17 +723,16 @@
             pltpu.VMEM((HEADS, WIDTH, 128), F32),
             pltpu.VMEM(by_head, BF16),
             pltpu.VMEM((STATE, ROWS), BF16),
-            pltpu.VMEM((RANKS, HEADS, 128), F32),
-            pltpu.VMEM((RANKS, HEADS, 128), F32),
+            pltpu.VMEM((RANKS, 1, STATE), F32),
+            pltpu.VMEM((RANKS, CHUNK + TAIL, STATE), BF16),
+            pltpu.VMEM((RANKS, CHUNK + TAIL, STATE), BF16),
             pltpu.VMEM(by_rank, BF16),
             pltpu.VMEM(by_rank, BF16),
             pltpu.VMEM(by_rank, BF16),
             pltpu.VMEM(by_rank, BF16),
             pltpu.VMEM(by_rank, BF16),
             pltpu.VMEM(by_rank, BF16),
-            pltpu.VMEM(by_rank, BF16),
-            pltpu.VMEM(by_rank, BF16),
-            pltpu.VMEM((2, 2, ROWS, CHANNELS), BF16),
+            pltpu.VMEM((2, ROWS, CHANNELS), BF16),
             pltpu.VMEM((4, 1, ROWS), F32),
             pltpu.VMEM((4, 1, ROWS), F32),
             pltpu.VMEM((RING, CHIP_ROWS, 128), F32),
@@ -756,8 +762,8 @@
             dma((16,)),
             dma((16,)),
             dma((16,)),
-            dma((5, RANKS)),
-            dma((5, RANKS)),
+            dma((4, RANKS)),
+            dma((4, RANKS)),
             dma((4, 4)),
             dma((4, 4)),
         ],

time: 69.7 us -> 65.5 us (0.940)
  Pallas kernels: 68.9 us -> 64.7 us
    pallas_call x1, Pallas kernels: 66.8 us -> 62.7 us  [on_device(): pl.pallas_call(layer, out_shape=[jax.ShapeDtypeStruct((OWN_ROWS, MODEL),...]
where the time goes in v3:
time: 65.5 us; the launch traced here: 65.4 us
  Pallas kernels  64.7 us (99%)
    pallas_call x1, Pallas kernels, on_device(): pl.pallas_call(layer, out_shape=[jax.ShapeDtypeStruct((OWN_ROWS, MODEL),...  62.7 us
    pallas_call x1, Pallas kernels, on_device(): pl.pallas_call(hand_out, out_shape=[jax.ShapeDtypeStruct(o.shape, o.dtype...  2.04 us

profile of v3, /device:TPU:1, one launch (start us, length us, event | category | flops | bytes accessed | tf_op | source)
XLA Modules:
  0.0 65.4 jit_solution(5560185919729883669)
XLA Ops:
  0.6 62.7 %layer.1 = (bf16[16,8192]{1,0:T(8,128)(2,1)}, bf16[256,512]{1,0:T(8,128)(2,1)}, bf16[256,512]{1,0:T(8,128)(2,1)}, bf16[64,256]{1,0:T(8,128)(2,1)}, bf16[64,256]{1,0:T(8,128)(2,1)}, /*index=5*/f32[8,256]{1,0:T(8,128)}) custom-call(bf16[256,512]{1,0:T(8,128)(2,1)} %x_hbm.1, bf16[256,512]{1,0:T(8,128)(2,1)} %gate_hbm.1, bf16[256,1024]{1,0:T(8,128)(2,1)} %b_hbm.1, ...), custom_call_target="tpu_custom_call" | custom-call | flops 6000000000 | bytes 16000000 | tf_op jit(solution)/shard_map/layer/pallas_call | solution.py:668
  63.3 2.0 %hand_out.1 = (bf16[16,8192]{1,0:T(8,128)(2,1)}, bf16[256,512]{1,0:T(8,128)(2,1)}, bf16[256,512]{1,0:T(8,128)(2,1)}, bf16[64,256]{1,0:T(8,128)(2,1)}, bf16[64,256]{1,0:T(8,128)(2,1)}, /*index=5*/f32[8,256]{1,0:T(8,128)}) custom-call(bf16[16,8192]{1,0:T(8,128)(2,1)} %get-tuple-element.18.refs_0_, bf16[256,512]{1,0:T(8,128)(2,1)} %get-tuple-element.19.refs_1_, ...), custom_call_target="tpu_custom_call" | custom-call | tf_op jit(solution)/shard_map/hand_out/pallas_call | solution.py:791

commit v4 on v3

--- a/solution.py
+++ b/solution.py
@@ -54,21 +54,16 @@
     w_hbm,
     docs_ref,
     go_hbm,
-    mixed_out,
-    gx_out,
-    gg_out,
-    gb_out,
-    gc_out,
-    gdt_out,
-    x_ref,
-    gate_ref,
-    dt_ref,
-    gain_ref,
+    mixed_ref,
     gx_ref,
     gg_ref,
     gb_ref,
     gc_ref,
     gdt_ref,
+    x_ref,
+    gate_ref,
+    dt_ref,
+    gain_ref,
     bv,
     cv,
     wv,
@@ -101,6 +96,7 @@
     rb2,
     eb2,
     zz,
+    sums,
     gn,
     nbuf,
     abuf,
@@ -124,7 +120,6 @@
     ob,
     orecv,
     loc,
-    out_s,
     pair_s,
     pair_r,
     ag_s,
@@ -313,6 +308,7 @@
     def keep_of(r):
         return keep[r]
 
+    ag_step(1, 0)
     each(1, RANKS, lambda k: ex_state(k).wait_recv())
     for r in range(RANKS):
         count = jnp.int32(0)
@@ -329,7 +325,6 @@
     each(1, RANKS, lambda k: ex_enter(k).start())
     s0[rank] = eb[rank]
 
-    ag_step(1, 0)
     mask[...] = jnp.where((seg_col == seg_row) & (row_ids <= col_ids), 0.0, -1e30)
     shifted = (running - jnp.log(step)).T
     for h in range(HEADS):
@@ -364,8 +359,9 @@
         gcol[2 * q : 2 * q + 2] = jnp.broadcast_to(column, (128, 128)).reshape(2, WIDTH, 128)
     cvt[...] = cv[...].T
 
+    ag_step(2, 0)
+
     each(1, RANKS, lambda k: ex_enter(k).wait_recv())
-    ag_step(2, 0)
     enter_all = s0[...].reshape(CHANNELS, STATE)
     car[...] = nt(enter_all, cv[...]).reshape(HEADS, WIDTH, ROWS)
 
@@ -457,22 +453,27 @@
     rs_step(0, 0)
 
     load_go.wait()
+
+    def fold(block):
+        total = jnp.zeros((CHIP_ROWS, 128), F32)
+        for n in range(HALF // tile):
+            cols = pl.ds(n * tile, tile)
+            part = gbuf[block, :, :, cols].reshape(CHIP_ROWS, tile).astype(F32)
+            both = part * pp[block, :, cols]
+            for i in range(tile // 128):
+                total = total + both[:, i * 128 : (i + 1) * 128]
+        sums[block] = total
+
+    def fold_far(d):
+        fold((chip + d) % RING)
+
+    each(0, 3, fold_far)
+    each(RING - 2, RING, fold_far)
     for way in range(2):
         for piece in range(2):
             ag_copy(3 if way == piece else 2, way, piece).wait_recv()
-
-    def fold(n, total):
-        cols = pl.ds(pl.multiple_of(n * tile, tile), tile)
-        both = gbuf[:, :, :, cols].reshape(ROWS, tile).astype(F32) * pp[:, :, cols].reshape(
-            ROWS, tile
-        )
-        for i in range(tile // 128):
-            total = total + both[:, i * 128 : (i + 1) * 128]
-        return total
-
-    along_col = jnp.sum(
-        lax.fori_loop(0, HALF // tile, fold, jnp.zeros((ROWS, 128), F32)), axis=1, keepdims=True
-    )
+    each(3, 6, fold_far)
+    along_col = jnp.sum(sums[...].reshape(ROWS, 128), axis=1, keepdims=True)
     abuf[0] = jnp.sum(jnp.where(eye, along_col, 0.0), axis=0, keepdims=True)
     for x in (1, 2, 3):
         mate_copy(1, abuf, x).start()
@@ -482,8 +483,8 @@
     qsend[...] = nt(wv[other], cotangent)
     pair_q = remote(qsend, qrecv, pair_s.at[3], pair_r.at[3], rank, sibling)
     pair_q.start()
+    grad_own = nt(wv[core], cotangent)
     rs_step(1, 0)
-    grad_own = nt(wv[core], cotangent)
     pair_q.wait_recv()
     grad_scaled = (grad_own + qrecv[...]).reshape(HEADS, WIDTH, ROWS) * gain_full
     for x in (1, 2, 3):
@@ -503,11 +504,6 @@
     rs_step(2, 1)
     gg_ref[...] = grad_gate.reshape(CHANNELS, ROWS).T
 
-    def leave(which, source, target):
-        return pltpu.make_async_copy(source, target, out_s.at[which])
-
-    leave_gg = leave(0, gg_ref, gg_out)
-    leave_gg.start()
 
     dgt[...] = jnp.zeros((ROWS, ROWS), F32)
 
@@ -578,13 +574,9 @@
         block = overlap[h * WIDTH : (h + 1) * WIDTH, :]
         inner = jnp.where(head_rows == h, jnp.sum(block), inner)
     gx_ref[...] = dxin[...].reshape(CHANNELS, ROWS).astype(BF16).T
-    leave_gx = leave(2, gx_ref, gx_out)
-    leave_gx.start()
     grad_rate = grad_rate + nn(zdot[...], before, HIGH) + kept * inner
     grad_step = (coldot[...] + zdot[...]) / step_s[...] + a_rate * grad_rate
     gdt_ref[...] = grad_step * (1.0 / (1.0 + jnp.exp(-raw)))
-    leave_dt = leave(3, gdt_ref, gdt_out)
-    leave_dt.start()
     for turn in (1, 0):
         for way in range(2):
             rs_copy(3, way, (way + turn) % 2).wait_recv()
@@ -598,12 +590,10 @@
         ob[:, :, cols] = value.astype(BF16).reshape(2, OWN_ROWS, PIECE)
     pair_out = remote(ob.at[other], orecv, pair_s.at[4], pair_r.at[4], rank, sibling)
     pair_out.start()
-    leave_mine = leave(1, ob.at[core], mixed_out.at[:, here])
-    leave_mine.start()
+    mixed_ref[:, here] = ob[core]
 
     pair_out.wait_recv()
-    leave_theirs = leave(4, orecv, mixed_out.at[:, there])
-    leave_theirs.start()
+    mixed_ref[:, there] = orecv[...]
 
     def gather(which):
         for x in (1, 2, 3):
@@ -614,11 +604,7 @@
         return shares.astype(BF16)
 
     gc_ref[...] = gather(1)
-    leave_gc = leave(5, gc_ref, gc_out)
-    leave_gc.start()
     gb_ref[...] = gather(0)
-    leave_gb = leave(6, gb_ref, gb_out)
-    leave_gb.start()
 
     for copy in (pair_go, pair_w, pair_gn, pair_q, pair_out):
         copy.wait_send()
@@ -636,8 +622,6 @@
         mate_copy(1, abuf, x).wait_send()
         share_copy(0, x).wait_send()
         share_copy(1, x).wait_send()
-    for copy in (leave_gg, leave_mine, leave_gx, leave_dt, leave_theirs, leave_gc, leave_gb):
-        copy.wait()
 
 
 def hand_out(*refs):
@@ -668,12 +652,12 @@
     out = pl.pallas_call(
         layer,
         out_shape=[
-            jax.ShapeDtypeStruct((OWN_ROWS, MODEL), BF16),
-            jax.ShapeDtypeStruct((ROWS, CHANNELS), BF16),
-            jax.ShapeDtypeStruct((ROWS, CHANNELS), BF16),
-            jax.ShapeDtypeStruct((WIDTH, ROWS), BF16),
-            jax.ShapeDtypeStruct((WIDTH, ROWS), BF16),
-            jax.ShapeDtypeStruct((HEADS, ROWS), F32),
+            pltpu.VMEM((OWN_ROWS, MODEL), BF16),
+            pltpu.VMEM((ROWS, CHANNELS), BF16),
+            pltpu.VMEM((ROWS, CHANNELS), BF16),
+            pltpu.VMEM((WIDTH, ROWS), BF16),
+            pltpu.VMEM((WIDTH, ROWS), BF16),
+            pltpu.VMEM((HEADS, ROWS), F32),
         ],
         in_specs=[
             anywhere,
@@ -689,17 +673,12 @@
             smem,
             anywhere,
         ],
-        out_specs=[anywhere] * 6,
+        out_specs=[vmem] * 6,
         scratch_shapes=[
             pltpu.VMEM((ROWS, CHANNELS), BF16),
             pltpu.VMEM((ROWS, CHANNELS), BF16),
             pltpu.VMEM((HEADS, ROWS), F32),
             pltpu.VMEM((1, CHANNELS), F32),
-            pltpu.VMEM((ROWS, CHANNELS), BF16),
-            pltpu.VMEM((ROWS, CHANNELS), BF16),
-            pltpu.VMEM((WIDTH, ROWS), BF16),
-            pltpu.VMEM((WIDTH, ROWS), BF16),
-            pltpu.VMEM((HEADS, ROWS), F32),
             pltpu.VMEM((ROWS, STATE), BF16),
             pltpu.VMEM((ROWS, STATE), BF16),
             pltpu.VMEM((2, CHANNELS, HALF), BF16),
@@ -732,6 +711,7 @@
             pltpu.VMEM(by_rank, BF16),
             pltpu.VMEM(by_rank, BF16),
             pltpu.VMEM(by_rank, BF16),
+            pltpu.VMEM((RING, CHIP_ROWS, 128), F32),
             pltpu.VMEM((2, ROWS, CHANNELS), BF16),
             pltpu.VMEM((4, 1, ROWS), F32),
             pltpu.VMEM((4, 1, ROWS), F32),
@@ -755,7 +735,6 @@
             pltpu.VMEM((2, OWN_ROWS, HALF), BF16),
             pltpu.VMEM((OWN_ROWS, HALF), BF16),
             dma((8,)),
-            dma((7,)),
             dma((5,)),
             dma((5,)),
             dma((16,)),
@@ -793,6 +772,7 @@
         out_shape=[jax.ShapeDtypeStruct(o.shape, o.dtype) for o in out],
         in_specs=[vmem] * 6,
         out_specs=[vmem] * 6,
+        compiler_params=pltpu.CompilerParams(vmem_limit_bytes=4 * 1024 * 1024),
         name="hand_out",
     )(*out)
     return (mixed, grad_x, grad_gate, grad_b.T, grad_c.T, grad_dt)

time: 65.5 us -> 62.8 us (0.959)
  Pallas kernels: 64.7 us -> 62 us
    pallas_call x1, Pallas kernels: 62.7 us -> 61 us  [on_device(): pl.pallas_call(layer, out_shape=[pltpu.VMEM((OWN_ROWS, MODEL), BF16), plt...]
    pallas_call x1, Pallas kernels: 2.04 us -> 0.95 us  [on_device(): pl.pallas_call(hand_out, out_shape=[jax.ShapeDtypeStruct(o.shape, o.dtype...]
where the time goes in v4:
time: 62.8 us; the launch traced here: 62.6 us
  Pallas kernels  62 us (99%)
  between operations  0.64 us (1%)
    pallas_call x1, Pallas kernels, on_device(): pl.pallas_call(layer, out_shape=[pltpu.VMEM((OWN_ROWS, MODEL), BF16), plt...  61 us

profile of v4, /device:TPU:1, one launch (start us, length us, event | category | flops | bytes accessed | tf_op | source)
XLA Modules:
  0.0 62.6 jit_solution(13760149308562594175)
XLA Ops:
  0.6 61.0 %layer.1 = (bf16[16,8192]{1,0:T(8,128)(2,1)S(1)}, bf16[256,512]{1,0:T(8,128)(2,1)S(1)}, bf16[256,512]{1,0:T(8,128)(2,1)S(1)}, bf16[64,256]{1,0:T(8,128)(2,1)S(1)...) custom-call(bf16[256,512]{1,0:T(8,128)(2,1)} %x_hbm.1, bf16[256,512]{1,0:T(8,128)(2,1)} %gate_hbm.1, ...), custom_call_target="tpu_custom_call" | custom-call | flops 6000000000 | bytes 16000000 | tf_op jit(solution)/shard_map/layer/pallas_call | solution.py:652
  61.7 0.9 %hand_out.1 = (bf16[16,8192]{1,0:T(8,128)(2,1)}, bf16[256,512]{1,0:T(8,128)(2,1)}, bf16[256,512]{1,0:T(8,128)(2,1)}, bf16[64,256]{1,0:T(8,128)(2,1)}, bf16[64,256]{1,0:T(8,128)(2,1)}, /*index=5*/f32[8,256]{1,0:T(8,128)}) custom-call(bf16[16,8192]{1,0:T(8,128)(2,1)S(1)} %get-tuple-element.18.refs_0_, bf16[256,512]{1,0:T(8,128)(2,1)S(1)} %get-tuple-element.19.refs_1_, ...), custom_call_target="tpu_custom_call" | custom-call | tf_op jit(solution)/shard_map/hand_out/pallas_call | solution.py:770
